TPU v7x, 128 devices: a whole 4x4x4 slice. The times are simulated.
128 devices in a mesh: flow: 16 (over z, y), group: 8 (over x, core).
Axes of the slice: x: 4, y: 4, z: 4, core: 2. Of those that a mesh axis runs over, the one named last changes fastest.
Arguments:
- cell_state: float32 [12, 524288], P(None, 'flow'), may hold values from 0.1 to 10
- inflow: float32 [12, 8192], P(None, ('flow', 'group')), may hold values from 0.1 to 10
- courant: float32 [256, 8192], P(None, ('flow', 'group')), may hold values from 1 to 15360
- pick: int32 [8, 16, 16, 1024], P('group', 'flow'), may hold values from 0 to 32767, as said below
- node_slot: int32 [256, 8192], P(None, ('flow', 'group')), may hold values from 0 to 16383, as said below
- stoich: float32 [6, 12], replicated, may hold values from 0 to 0.25
- logk: float32 [6], replicated, may hold values from -3 to 0
Outputs:
- cell_species: float32 [18, 524288], P(None, ('flow', 'group'))
Inputs may be any that keep to these rules, and one draw needn't show every extreme that they name: pick[g, a, b, k] lies in the block of 128 local cells numbered ((b * 1024 + k) // 128 + g * 128) modulo (256). With j = s % 64, node_slot[n, s] lies in the tile of 128 records numbered (n * 64 + j) // 128.
All inputs are finite; a program needn't handle non-finite values.
Results may differ from a plain program's by a relative error of at most 0.00011.
Values sent between devices are 32-bit elements; how exact they have to be, the bound alone decides.
No kernel may reach another device: no remote copies, remote signals or barrier semaphores. Data moves between devices by JAX's collectives and lax.ppermute only.
A program may use at most 128 MiB of HBM per device.

v0:
```python
import jax
import jax.numpy as jnp
from jax import lax
from jax.sharding import PartitionSpec as P

ITERS = 4
WIN = 128


def solve_spd(matrix, rhs):
    order = len(rhs)
    lower = {}
    inverse = []
    for outer in range(order):
        for inner in range(outer + 1):
            total = matrix[outer, inner]
            for other in range(inner):
                total = total - lower[outer, other] * lower[inner, other]
            if outer == inner:
                inverse.append(lax.rsqrt(total))
            else:
                lower[outer, inner] = total * inverse[inner]
    middle = []
    for outer in range(order):
        total = rhs[outer]
        for other in range(outer):
            total = total - lower[outer, other] * middle[other]
        middle.append(total * inverse[outer])
    result = [None] * order
    for outer in reversed(range(order)):
        total = middle[outer]
        for other in range(outer + 1, order):
            total = total - lower[other, outer] * result[other]
        result[outer] = total * inverse[outer]
    return result


def speciate(totals, stoich, logk):
    count_comp = totals.shape[0]
    identity = jnp.eye(count_comp, dtype=jnp.float32)
    logfree = jnp.log(totals)
    for sweep in range(ITERS):
        free = jnp.exp(logfree)
        complexes = jnp.exp(
            logk[:, None]
            + jnp.dot(
                stoich, logfree, precision=lax.Precision.HIGHEST, preferred_element_type=jnp.float32
            )
        )
        mismatch = (
            free
            + jnp.dot(
                stoich.T,
                complexes,
                precision=lax.Precision.HIGHEST,
                preferred_element_type=jnp.float32,
            )
            - totals
        )
        jacobian = jnp.einsum(
            "pi,pj,pn->ijn", stoich, stoich, complexes, precision=lax.Precision.HIGHEST
        )
        jacobian = jacobian + identity[:, :, None] * free[:, None, :]
        update = solve_spd(jacobian, [-mismatch[comp] for comp in range(count_comp)])
        logfree = logfree + jnp.stack(update)
    complexes = jnp.exp(
        logk[:, None]
        + jnp.dot(
            stoich, logfree, precision=lax.Precision.HIGHEST, preferred_element_type=jnp.float32
        )
    )
    return jnp.concatenate([jnp.exp(logfree), complexes], axis=0)


def compose_nodes(earlier, later):
    return (later[0] * earlier[0], later[0][:, None, :] * earlier[1] + later[1])


def one_hot_tiles(local, window):
    positions = lax.broadcasted_iota(jnp.int32, (1, window, 1), 1)
    return (local[:, None, :] == positions).astype(jnp.float32)


def body(cell_state, inflow, courant, pick, node_slot, stoich, logk):
    count_comp, cell_count = cell_state.shape
    node_count, lines = courant.shape
    flow_count = lax.axis_size("flow")
    capacity = pick.shape[3]
    slot_total = flow_count * capacity
    tile_count = slot_total // WIN
    block_count = cell_count // WIN
    used = min(tile_count, block_count)
    repeat = tile_count // used
    offset = lax.axis_index("group") * tile_count % block_count
    pick_table = one_hot_tiles(pick.reshape(tile_count, WIN) % WIN, WIN)
    node_table = one_hot_tiles(node_slot.reshape(tile_count, WIN) % WIN, WIN)
    cell_blocks = cell_state.reshape(count_comp, block_count, WIN)
    doubled = jnp.concatenate([cell_blocks, cell_blocks], axis=1)
    chosen = lax.dynamic_slice_in_dim(doubled, offset, used, 1)
    chosen = jnp.tile(chosen, (1, repeat, 1))
    outgoing = jnp.einsum("ctl,tlr->ctr", chosen, pick_table, precision=lax.Precision.HIGHEST)
    incoming = lax.all_to_all(
        outgoing.reshape(count_comp, flow_count, capacity),
        "flow",
        split_axis=1,
        concat_axis=1,
        tiled=True,
    )
    records = incoming.reshape(count_comp, tile_count, WIN)
    old = jnp.einsum("ctl,tln->ctn", records, node_table, precision=lax.Precision.HIGHEST)
    old = old.reshape(count_comp, node_count, lines)
    weight = courant / (1.0 + courant)
    source = jnp.transpose(old / (1.0 + courant)[None], (1, 0, 2))
    running_scale, running_offset = lax.associative_scan(compose_nodes, (weight, source), axis=0)
    moved = running_scale[:, None, :] * inflow[None] + running_offset
    moved = jnp.transpose(moved, (1, 0, 2)).reshape(count_comp, node_count * lines)
    species = speciate(moved, stoich, logk)
    width = species.shape[0]
    species_tiles = species.reshape(width, tile_count, WIN)
    slot_sums = jnp.einsum(
        "qtn,tln->qtl", species_tiles, node_table, precision=lax.Precision.HIGHEST
    )
    slot_counts = jnp.sum(node_table, axis=2)[None]
    back_sums, back_counts = (
        lax.all_to_all(
            slot_sums.reshape(width, flow_count, capacity),
            "flow",
            split_axis=1,
            concat_axis=1,
            tiled=True,
        ),
        lax.all_to_all(
            slot_counts.reshape(1, flow_count, capacity),
            "flow",
            split_axis=1,
            concat_axis=1,
            tiled=True,
        ),
    )
    returned = jnp.concatenate(
        [back_sums.reshape(width, tile_count, WIN), back_counts.reshape(1, tile_count, WIN)], axis=0
    )
    placed = jnp.einsum("qtr,tlr->qtl", returned, pick_table, precision=lax.Precision.HIGHEST)
    placed = jnp.sum(placed.reshape(width + 1, repeat, used, WIN), axis=1)
    buffer = jnp.zeros((width + 1, 2 * block_count, WIN), jnp.float32)
    buffer = lax.dynamic_update_slice_in_dim(buffer, placed, offset, 1)
    folded = (buffer[:, :block_count] + buffer[:, block_count:]).reshape(width + 1, cell_count)
    cell_sums = folded[:width]
    cell_counts = folded[width:]
    full_sums, full_counts = lax.psum((cell_sums, cell_counts), "group")
    block = cell_count // lax.axis_size("group")
    begin = lax.axis_index("group") * block
    own_sums = lax.dynamic_slice_in_dim(full_sums, begin, block, 1)
    own_counts = lax.dynamic_slice_in_dim(full_counts, begin, block, 1)
    return own_sums / jnp.maximum(own_counts, 1.0)


def solution(mesh):
    placed = (
        P(None, "flow"),
        P(None, ("flow", "group")),
        P(None, ("flow", "group")),
        P("group", "flow", None, None),
        P(None, ("flow", "group")),
        P(),
        P(),
    )
    return jax.shard_map(
        body, mesh=mesh, in_specs=placed, out_specs=P(None, ("flow", "group")), check_vma=False
    )
```

profile of v0, /device:TPU:0, one launch (start us, length us, event | category | flops | bytes accessed | tf_op | source)
XLA Modules:
  0.0 394.2 jit_solution(7408837176598221739)
XLA Ops:
  6.5 0.9 reshape.32825
  7.4 2.0 copy.73
  9.6 0.9 copy.57
  10.5 4.1 %fusion.36 = f32[12,128,128]{2,0,1:T(8,128)S(1)} fusion(s32[128,128]{1,0:T(8,128)S(1)} %add_select_fusion.1, s32[]{:T(128)S(6)} %select_n.36, f32[12,256,128]{2,0,1:T(8,128)S(1)} %copy.57), kind=kOutput, calls=%fused_computation.54 | convolution fusion | flops 304283648 | bytes 2424836 | tf_op jit(solution)/shard_map/ctl,tlr->ctr/dot_general | solution.py:101
  15.1 1.5 copy.60
  16.6 8.5 %all-to-all-start = ((f32[12,16,1024]{2,0,1:T(8,128)}), f32[12,16,1024]{2,0,1:T(8,128)S(1)}, u32[]{:S(2)}, u32[]{:S(2)}) async-start(f32[12,16,1024]{2,0,1:T(8,128)} %copy.60), calls=%async_computation | async-start | bytes 2097152 | tf_op jit(solution)/shard_map/all_to_all | solution.py:102
  29.6 13.1 %all-to-all-done = f32[12,16,1024]{2,0,1:T(8,128)S(1)} async-done(((f32[12,16,1024]{2,0,1:T(8,128)}), f32[12,16,1024]{2,0,1:T(8,128)S(1)}, u32[]{:S(2)}, u32[]{:S(2)}) %all-to-all-start) | async-done | bytes 786464 | tf_op jit(solution)/shard_map/all_to_all | solution.py:102
  43.3 4.1 %fusion.37 = f32[12,128,128]{2,0,1:T(8,128)S(1)} fusion(s32[128,128]{1,0:T(8,128)S(1)} %add_select_fusion, f32[12,128,128]{2,1,0:T(8,128)S(1)} %reshape.32829), kind=kOutput, calls=%fused_computation.55 | convolution fusion | flops 304087040 | bytes 1638400 | tf_op jit(solution)/shard_map/ctl,tln->ctn/dot_general | solution.py:110
  48.4 2.1 slice.1367
  50.5 1.2 multiply_add_fusion
  52.1 0.8 multiply_add_fusion.1
  53.2 0.7 multiply_add_fusion.2
  54.0 0.7 multiply_add_fusion.3
  57.4 2.1 slice.1401
  62.5 1.0 add.328
  63.4 5.3 %pad.129 = f32[256,12,64]{2,0,1:T(8,128)S(1)} pad(f32[128,12,64]{2,0,1:T(8,128)} %add.328, f32[]{:T(128)} %constant.38.clone.1), padding=1_0_1x0_0_0x0_0_0 | pad | bytes 1179652 | tf_op jit(solution)/shard_map/pad | solution.py:114
  68.8 1.3 fusion.42
  70.1 1.0 pad_maximum_fusion.1
  71.1 5.8 %pad.128 = f32[256,12,64]{2,0,1:T(8,128)S(1)} pad(f32[128,12,64]{2,0,1:T(8,128)} %pad_maximum_fusion.1, f32[]{:T(128)} %constant.38.clone.1), padding=0_1_1x0_0_0x0_0_0 | pad | bytes 1179652 | tf_op jit(solution)/shard_map/pad | solution.py:114
  76.9 1.4 add_bitcast_fusion
  78.3 1.9 reshape.32831
  80.5 0.9 fusion.17
  81.4 1.2 fusion.11
  82.6 12.8 %fusion = f32[12,12,16384]{2,0,1:T(8,128)S(1)} fusion(f32[12,16384]{1,0:T(8,128)S(1)} %log_exponential_fusion, f32[12,12]{0,1:T(8,128)S(1)} %copy-done.9, f32[16384,6]{0,1:T(8,128)S(1)} %fusion.17, f32[6,12]{1,0:T(8,128)S(1)} %copy-done, f32[6,12]{0,1:T(8,128)S(1)} %copy.64), kind=kOutput, calls=%fused_computation.4 | convolution fusion | flops 174588768 | bytes 10617984 | tf_op jit(solution)/shard_map/pi,pj,pn->ijn/dot_general | solution.py:60
  95.5 13.7 %subtract_multiply_fusion.159 = (f32[1,16384]{1,0:T(1,128)S(1)}, f32[1,16384]{1,0:T(1,128)S(1)}, f32[1,16384]{1,0:T(1,128)S(1)}, f32[1,16384]{1,0:T(1,128)S(1)},...) fusion(f32[12,16384]{1,0:T(8,128)S(1)} %fusion.11, ...), kind=kLoop, calls=%fused_computation.1528 | loop fusion | flops 10272768 | bytes 9830400 | tf_op jit(solution)/shard_map/mul | solution.py:28
  109.2 4.4 %subtract_multiply_fusion.152 = (f32[1,16384]{1,0:T(1,128)S(1)}, f32[1,16384]{1,0:T(1,128)S(1)}, f32[1,16384]{1,0:T(1,128)S(1)}, f32[1,16384]{1,0:T(1,128)S(1)},...) fusion(f32[1,16384]{1,0:T(1,128)S(1)} %get-tuple-element.322, ...), kind=kLoop, calls=%fused_computation.1520 | loop fusion | flops 2310144 | bytes 5767168 | tf_op jit(solution)/shard_map/mul | solution.py:22
  113.6 6.5 %subtract_multiply_fusion.141 = (f32[1,16384]{1,0:T(1,128)}, f32[1,16384]{1,0:T(1,128)}, f32[1,16384]{1,0:T(1,128)}, f32[1,16384]{1,0:T(1,128)}, f32[1,16384]{1,...) fusion(f32[1,16384]{1,0:T(1,128)S(1)} %get-tuple-element.394, ...), kind=kLoop, calls=%fused_computation.1509 | loop fusion | flops 3440640 | bytes 6684672 | tf_op jit(solution)/shard_map/mul | solution.py:34
  120.1 2.9 stack.8
  123.3 1.0 fusion.16
  124.3 1.2 fusion.9
  125.5 12.8 %fusion.1 = f32[12,12,16384]{2,0,1:T(8,128)S(1)} fusion(f32[12,16384]{1,0:T(8,128)S(1)} %fusion.1002, f32[12,12]{0,1:T(8,128)S(1)} %copy-done.10, f32[16384,6]{0,1:T(8,128)S(1)} %fusion.16, f32[6,12]{1,0:T(8,128)S(1)} %copy-done, f32[6,12]{0,1:T(8,128)S(1)} %copy.64), kind=kOutput, calls=%fused_computation.5 | convolution fusion | flops 174588768 | bytes 10617984 | tf_op jit(solution)/shard_map/pi,pj,pn->ijn/dot_general | solution.py:60
  138.3 13.8 %subtract_multiply_fusion.112 = (f32[1,16384]{1,0:T(1,128)S(1)}, f32[1,16384]{1,0:T(1,128)S(1)}, f32[1,16384]{1,0:T(1,128)S(1)}, f32[1,16384]{1,0:T(1,128)S(1)},...) fusion(f32[12,16384]{1,0:T(8,128)S(1)} %fusion.9, ...), kind=kLoop, calls=%fused_computation.1474 | loop fusion | flops 10272768 | bytes 9830400 | tf_op jit(solution)/shard_map/mul | solution.py:28
  152.1 4.2 %subtract_multiply_fusion.105 = (f32[1,16384]{1,0:T(1,128)S(1)}, f32[1,16384]{1,0:T(1,128)S(1)}, f32[1,16384]{1,0:T(1,128)S(1)}, f32[1,16384]{1,0:T(1,128)S(1)},...) fusion(f32[1,16384]{1,0:T(1,128)S(1)} %get-tuple-element.226, ...), kind=kLoop, calls=%fused_computation.1466 | loop fusion | flops 2310144 | bytes 5767168 | tf_op jit(solution)/shard_map/mul | solution.py:22
  156.3 6.5 %subtract_multiply_fusion.94 = (f32[1,16384]{1,0:T(1,128)}, f32[1,16384]{1,0:T(1,128)}, f32[1,16384]{1,0:T(1,128)}, f32[1,16384]{1,0:T(1,128)}, f32[1,16384]{1,0...) fusion(f32[1,16384]{1,0:T(1,128)S(1)} %get-tuple-element.298, ...), kind=kLoop, calls=%fused_computation.1455 | loop fusion | flops 3440640 | bytes 6684672 | tf_op jit(solution)/shard_map/mul | solution.py:34
  162.8 4.6 %stack.9 = f32[12,16384]{1,0:T(8,128)} concatenate(f32[1,16384]{1,0:T(1,128)} %get-tuple-element.203, f32[1,16384]{1,0:T(1,128)} %get-tuple-element.204, f32[1,16384]{1,0:T(1,128)} %get-tuple-element.205, f32[1,16384]{1,0:T(1,128)} %get-tuple-element.206, f32[1,16384]{1,0:T(1,128)} %get-tuple-element.207, f32[1,16384]{1,0:T(1,128)} %get-tuple-element.208, ...), dimensions={0} | concatenate | bytes 1572864 | tf_op jit(solution)/shard_map/stack | solution.py:65
  167.4 1.5 fusion.1090
  168.9 0.7 fusion.15
  169.7 1.1 fusion.7
  170.8 12.8 %fusion.2 = f32[12,12,16384]{2,0,1:T(8,128)S(1)} fusion(f32[12,16384]{1,0:T(8,128)S(1)} %get-tuple-element.201, f32[12,12]{0,1:T(8,128)S(1)} %copy-done.11, f32[16384,6]{0,1:T(8,128)S(1)} %fusion.15, f32[6,12]{1,0:T(8,128)S(1)} %copy-done, f32[6,12]{0,1:T(8,128)S(1)} %copy.64), kind=kOutput, calls=%fused_computation.6 | convolution fusion | flops 174588768 | bytes 10617984 | tf_op jit(solution)/shard_map/pi,pj,pn->ijn/dot_general | solution.py:60
  183.6 13.9 %subtract_multiply_fusion.65 = (f32[1,16384]{1,0:T(1,128)S(1)}, f32[1,16384]{1,0:T(1,128)S(1)}, f32[1,16384]{1,0:T(1,128)S(1)}, f32[1,16384]{1,0:T(1,128)S(1)}, ...) fusion(f32[12,16384]{1,0:T(8,128)S(1)} %fusion.7, ...), kind=kLoop, calls=%fused_computation.1420 | loop fusion | flops 10272768 | bytes 9830400 | tf_op jit(solution)/shard_map/mul | solution.py:28
  197.5 4.1 %subtract_multiply_fusion.58 = (f32[1,16384]{1,0:T(1,128)S(1)}, f32[1,16384]{1,0:T(1,128)S(1)}, f32[1,16384]{1,0:T(1,128)S(1)}, f32[1,16384]{1,0:T(1,128)S(1)}, ...) fusion(f32[1,16384]{1,0:T(1,128)S(1)} %get-tuple-element.128, ...), kind=kLoop, calls=%fused_computation.1412 | loop fusion | flops 2310144 | bytes 5767168 | tf_op jit(solution)/shard_map/mul | solution.py:22
  201.7 6.5 %subtract_multiply_fusion.47 = (f32[1,16384]{1,0:T(1,128)}, f32[1,16384]{1,0:T(1,128)}, f32[1,16384]{1,0:T(1,128)}, f32[1,16384]{1,0:T(1,128)}, f32[1,16384]{1,0...) fusion(f32[1,16384]{1,0:T(1,128)S(1)} %get-tuple-element.200, ...), kind=kLoop, calls=%fused_computation.1401 | loop fusion | flops 3440640 | bytes 6684672 | tf_op jit(solution)/shard_map/mul | solution.py:34
  208.2 4.2 %stack.10 = f32[12,16384]{1,0:T(8,128)} concatenate(f32[1,16384]{1,0:T(1,128)} %get-tuple-element.105, f32[1,16384]{1,0:T(1,128)} %get-tuple-element.106, f32[1,16384]{1,0:T(1,128)} %get-tuple-element.107, f32[1,16384]{1,0:T(1,128)} %get-tuple-element.108, f32[1,16384]{1,0:T(1,128)} %get-tuple-element.109, f32[1,16384]{1,0:T(1,128)} %get-tuple-element.110, ...), dimensions={0} | concatenate | bytes 1572864 | tf_op jit(solution)/shard_map/stack | solution.py:65
  212.4 1.4 fusion.1046
  213.8 0.7 fusion.14
  214.5 1.1 fusion.5
  215.7 13.0 %fusion.3 = f32[12,12,16384]{2,0,1:T(8,128)S(1)} fusion(f32[12,16384]{1,0:T(8,128)S(1)} %get-tuple-element.103, f32[12,12]{0,1:T(8,128)S(1)} %copy-done.12, f32[16384,6]{0,1:T(8,128)S(1)} %fusion.14, f32[6,12]{1,0:T(8,128)S(1)} %copy-done, f32[6,12]{0,1:T(8,128)S(1)} %copy.64), kind=kOutput, calls=%fused_computation.7 | convolution fusion | flops 174588768 | bytes 10617984 | tf_op jit(solution)/shard_map/pi,pj,pn->ijn/dot_general | solution.py:60
  228.7 13.8 %subtract_multiply_fusion.18 = (f32[1,16384]{1,0:T(1,128)S(1)}, f32[1,16384]{1,0:T(1,128)S(1)}, f32[1,16384]{1,0:T(1,128)S(1)}, f32[1,16384]{1,0:T(1,128)S(1)}, ...) fusion(f32[12,16384]{1,0:T(8,128)S(1)} %fusion.5, ...), kind=kLoop, calls=%fused_computation.1366 | loop fusion | flops 10272768 | bytes 9830400 | tf_op jit(solution)/shard_map/mul | solution.py:28
  242.5 4.2 %subtract_multiply_fusion.11 = (f32[1,16384]{1,0:T(1,128)S(1)}, f32[1,16384]{1,0:T(1,128)S(1)}, f32[1,16384]{1,0:T(1,128)S(1)}, f32[1,16384]{1,0:T(1,128)S(1)}, ...) fusion(f32[1,16384]{1,0:T(1,128)S(1)} %get-tuple-element.30, ...), kind=kLoop, calls=%fused_computation.1358 | loop fusion | flops 2310144 | bytes 5767168 | tf_op jit(solution)/shard_map/mul | solution.py:22
  246.6 6.5 %subtract_multiply_fusion = (f32[1,16384]{1,0:T(1,128)}, f32[1,16384]{1,0:T(1,128)}, f32[1,16384]{1,0:T(1,128)}, f32[1,16384]{1,0:T(1,128)}, f32[1,16384]{1,0:T(...) fusion(f32[1,16384]{1,0:T(1,128)S(1)} %get-tuple-element.102, ...), kind=kLoop, calls=%fused_computation.1347 | loop fusion | flops 3440640 | bytes 6684672 | tf_op jit(solution)/shard_map/mul | solution.py:34
  253.2 3.1 stack.11
  256.5 0.9 fusion.13
  258.3 6.6 %fusion.30 = f32[18,128,128]{2,0,1:T(8,128)S(1)} fusion(f32[18,128,128]{2,1,0:T(8,128)S(1)} %slice.2170, s32[128,128]{1,0:T(8,128)S(1)} %copy-done.8), kind=kOutput, calls=%fused_computation.52 | convolution fusion | flops 455081984 | bytes 2424832 | tf_op jit(solution)/shard_map/qtn,tln->qtl/dot_general | solution.py:120
  265.4 1.9 copy.67
  267.2 3.7 all-to-all-start.1
  271.0 2.0 convert_reduce_fusion
  272.9 20.3 %all-to-all-done.1 = f32[18,16,1024]{2,0,1:T(8,128)S(1)} async-done(((f32[18,16,1024]{2,0,1:T(8,128)}), f32[18,16,1024]{2,0,1:T(8,128)S(1)}, u32[]{:S(2)}, u32[]{:S(2)}) %all-to-all-start.1) | async-done | bytes 1179680 | tf_op jit(solution)/shard_map/all_to_all | solution.py:125
  293.3 3.5 all-to-all-start.2
  298.7 5.7 %all-to-all-done.2 = f32[1,16,1024]{2,0,1:T(1,128)S(1)} async-done(((f32[1,16,1024]{2,0,1:T(1,128)}), f32[1,16,1024]{2,0,1:T(1,128)S(1)}, u32[]{:S(2)}, u32[]{:S(2)}) %all-to-all-start.2) | async-done | bytes 65568 | tf_op jit(solution)/shard_map/all_to_all | solution.py:132
  304.4 6.6 %fusion.33 = f32[19,128,128]{2,0,1:T(8,128)S(1)} fusion(f32[1,128,128]{2,0,1:T(1,128)S(1)} %bitcast.3483, f32[18,128,128]{2,0,1:T(8,128)S(1)} %copy.69, s32[128,128]{1,0:T(8,128)S(1)} %copy-done.22), kind=kOutput, calls=%fused_computation.53 | convolution fusion | flops 480559104 | bytes 2555904 | tf_op jit(solution)/shard_map/qtr,tlr->qtl/dot_general | solution.py:143
  313.5 3.5 copy.75
  317.0 67.4 %all-reduce.35.cloned.1.call-done = (f32[18,32768]{1,0:T(8,128)}, f32[1,32768]{1,0:T(1,128)}) async-done(((f32[18,32768]{1,0:T(8,128)}, f32[1,32768]{1,0:T(1,128)}), (f32[18,32768]{1,0:T(8,128)}, f32[1,32768]{1,0:T(1,128)})) %all-reduce.35.cloned.1.call-update) | async-done | bytes 2490384 | tf_op jit(solution)/shard_map/psum | solution.py:150
  384.4 0.7 dynamic-slice_maximum_fusion
  385.1 1.8 dynamic-slice_divide_fusion
  (235 shorter events, 18.5 us)
Async XLA Ops:
  7.4 3.1 copy-start.21
  15.0 10.1 %copy-start.19 = (f32[256,64]{0,1:T(8,128)S(1)}, f32[256,64]{0,1:T(8,128)}, u32[]{:S(2)}) copy-start(f32[256,64]{0,1:T(8,128)} %param.9) | copy-start | bytes 196612
  16.6 11.4 %copy-start.20 = (s32[256,64]{0,1:T(8,128)S(1)}, s32[256,64]{0,1:T(8,128)}, u32[]{:S(2)}) copy-start(s32[256,64]{0,1:T(8,128)} %param.11) | copy-start | bytes 196612
  16.6 26.1 %all-to-all-start = ((f32[12,16,1024]{2,0,1:T(8,128)}), f32[12,16,1024]{2,0,1:T(8,128)S(1)}, u32[]{:S(2)}, u32[]{:S(2)}) async-start(f32[12,16,1024]{2,0,1:T(8,128)} %copy.60), calls=%async_computation | async-start | bytes 2097152 | tf_op jit(solution)/shard_map/all_to_all | solution.py:102
  25.1 3.1 copy-start
  25.3 2.5 copy-start.4
  25.4 2.4 copy-start.13
  25.4 2.2 copy-start.16
  25.5 2.0 copy-start.23
  25.6 0.6 copy-start.28
  26.1 1.4 copy-start.30
  26.2 1.3 copy-start.26
  26.2 1.5 copy-start.17
  26.3 1.6 copy-start.14
  26.3 1.5 copy-start.5
  27.8 15.5 %copy-start.1 = (f32[127,64]{1,0:T(8,128)}, f32[127,64]{1,0:T(8,128)S(1)}, u32[]{:S(2)}) copy-start(f32[127,64]{1,0:T(8,128)S(1)} %slice.1329) | copy-start | bytes 97540
  29.6 17.8 %copy-start.7 = (s32[128,128]{1,0:T(8,128)}, s32[128,128]{1,0:T(8,128)S(1)}, u32[]{:S(2)}) copy-start(s32[128,128]{1,0:T(8,128)S(1)} %add_select_fusion) | copy-start | bytes 196612
  53.2 6.9 %copy-start.31 = (f32[2,64]{1,0:T(2,128)S(1)}, f32[2,64]{1,0:T(2,128)}, u32[]{:S(2)}) copy-start(f32[2,64]{1,0:T(2,128)} %copy-done.30) | copy-start | bytes 1540
  53.2 6.9 %copy-start.34 = (f32[64]{0:T(128)S(1)}, f32[64]{0:T(128)}, u32[]{:S(2)}) copy-start(f32[64]{0:T(128)} %get-tuple-element.405) | copy-start | bytes 772
  53.2 7.1 %copy-start.33 = (f32[64]{0:T(128)S(1)}, f32[64]{0:T(128)}, u32[]{:S(2)}) copy-start(f32[64]{0:T(128)} %get-tuple-element.402) | copy-start | bytes 772
  54.0 6.6 %copy-start.27 = (f32[3,64]{1,0:T(4,128)S(1)}, f32[3,64]{1,0:T(4,128)}, u32[]{:S(2)}) copy-start(f32[3,64]{1,0:T(4,128)} %copy-done.26) | copy-start | bytes 2308
  55.5 5.5 %copy-start.18 = (f32[15,64]{1,0:T(8,128)S(1)}, f32[15,64]{1,0:T(8,128)}, u32[]{:S(2)}) copy-start(f32[15,64]{1,0:T(8,128)} %copy-done.17) | copy-start | bytes 11524
  57.4 4.2 %copy-start.15 = (f32[31,64]{1,0:T(8,128)S(1)}, f32[31,64]{1,0:T(8,128)}, u32[]{:S(2)}) copy-start(f32[31,64]{1,0:T(8,128)} %copy-done.14) | copy-start | bytes 23812
  61.1 0.8 copy-start.6
  61.4 0.7 copy-start.25
  62.5 6.3 %copy-start.2 = (f32[127,64]{1,0:T(8,128)S(1)}, f32[127,64]{1,0:T(8,128)}, u32[]{:S(2)}) copy-start(f32[127,64]{1,0:T(8,128)} %copy-done.1) | copy-start | bytes 97540
  63.4 6.6 %copy-start.24 = (f32[1,12,64]{2,0,1:T(1,128)S(1)}, f32[1,12,64]{2,0,1:T(1,128)}, u32[]{:S(2)}) copy-start(f32[1,12,64]{2,0,1:T(1,128)} %slice.1781) | copy-start | bytes 9220
  70.0 6.8 %copy-start.3 = (f32[256,64]{1,0:T(8,128)S(1)}, f32[256,64]{1,0:T(8,128)}, u32[]{:S(2)}) copy-start(f32[256,64]{1,0:T(8,128)} %add.305) | copy-start | bytes 196612
  70.1 6.8 %copy-start.32 = (f32[12,64]{1,0:T(8,128)S(1)}, f32[12,64]{1,0:T(8,128)}, u32[]{:S(2)}) copy-start(f32[12,64]{1,0:T(8,128)} %param.8) | copy-start | bytes 9220
  78.3 2.2 copy-start.29
  80.5 2.1 copy-start.9
  124.3 1.2 copy-start.10
  168.9 1.9 copy-start.11
  213.8 1.9 copy-start.12
  257.5 0.8 copy-start.8
  267.2 26.0 %all-to-all-start.1 = ((f32[18,16,1024]{2,0,1:T(8,128)}), f32[18,16,1024]{2,0,1:T(8,128)S(1)}, u32[]{:S(2)}, u32[]{:S(2)}) async-start(f32[18,16,1024]{2,0,1:T(8,128)} %copy.67), calls=%async_computation.1 | async-start | bytes 3145728 | tf_op jit(solution)/shard_map/all_to_all | solution.py:125
  293.3 11.1 %all-to-all-start.2 = ((f32[1,16,1024]{2,0,1:T(1,128)}), f32[1,16,1024]{2,0,1:T(1,128)S(1)}, u32[]{:S(2)}, u32[]{:S(2)}) async-start(f32[1,16,1024]{2,0,1:T(1,128)} %bitcast.332), calls=%async_computation.2 | async-start | bytes 131072 | tf_op jit(solution)/shard_map/all_to_all | solution.py:132
  296.8 87.6 %all-reduce.35.cloned.1.call-start = ((), (), s32[]{:S(2)}) async-start(), calls=%async_computation.3 | async-start | bytes 6553600 | tf_op jit(solution)/shard_map/psum | solution.py:150
  297.8 6.6 %copy-start.22 = (s32[128,128]{1,0:T(8,128)S(1)}, s32[128,128]{1,0:T(8,128)}, u32[]{:S(2)}) copy-start(s32[128,128]{1,0:T(8,128)} %copy-done.21) | copy-start | bytes 196612
Sparse Core Ops, SparseCore 0:
  317.1 67.2 all-reduce.34
where the time goes:
time: 402 us; the launch traced here: 394 us
  other arithmetic  118 us (29%)
  waiting for transfers between devices  107 us (27%)
  matrix products  81.8 us (20%)
  local copies, waits for them, and re-layouts  56 us (14%)
  starting transfers between devices  16 us (4%)
  between operations  15.4 us (4%)
    psum x1, waiting for transfers between devices, body(): full_sums, full_counts = lax.psum((cell_sums, cell_counts), 'group')  67.4 us
    mul x4, other arithmetic, solve_spd(): middle.append(total * inverse[outer])  55.1 us
    dot_general x4, matrix products, speciate(): jnp.einsum('pi,pj,pn->ijn', stoich, stoich, complexes, precision=lax.Prec...  51.5 us
    mul x4, other arithmetic, solve_spd(): result[outer] = total * inverse[outer]  26.1 us
    all_to_all x1, waiting for transfers between devices, body(): lax.all_to_all(slot_sums.reshape(width, flow_count, capacity), 'flow', sp...  20.3 us
    mul x4, other arithmetic, solve_spd(): lower[outer, inner] = total * inverse[inner]  16.8 us
    another operation x4, local copies, waits for them, and re-layouts, speciate(): logfree = logfree + jnp.stack(update)  14.8 us
    all_to_all x1, waiting for transfers between devices, body(): lax.all_to_all(outgoing.reshape(count_comp, flow_count, capacity), 'flow'...  13.1 us
  transfers between devices with their start and end apart: 4, of which 4 were waited for; matrix products, arithmetic and copies ran while one was open for 2% of the time, Pallas kernels for 0%

commit v1 on v0

v1 whole, which is shorter than its diff:
```python
import functools

import jax
import jax.numpy as jnp
from jax import lax
from jax.experimental import pallas as pl
from jax.experimental.pallas import tpu as pltpu
from jax.sharding import Mesh, PartitionSpec as P

ITERS = 4
WIN = 128
NC = 12
NX = 6
NQ = NC + NX + 1
PAD = 24
SIDE = 4
FLOW = 16
SUB = 8
HALF = 64
BATCH = 8
BF16 = jnp.bfloat16
F32 = jnp.float32


def split(value, parts):
    out = []
    for part in range(parts):
        out.append(value.astype(BF16))
        if part < parts - 1:
            value = value - out[-1].astype(F32)
    return out


def dot(left, right):
    return jnp.dot(left, right, preferred_element_type=F32)


ALL = [(0, 0), (0, 1), (0, 2), (1, 0), (1, 1), (2, 0)]
MOST = ALL[:5]


def stack(parts, terms):
    return jnp.concatenate([parts[right] for _, right in terms], axis=0)


def tables(stoich):
    eye = jnp.eye(SUB, dtype=F32)

    def table(small, terms):
        rows, columns = small.shape
        value = small[:, None, :, None] * eye[None, :, None, :]
        value = value.reshape(rows * SUB, columns * SUB)
        parts = []
        for _ in range(3):
            part = lax.reduce_precision(value, 8, 7)
            parts.append(part.astype(BF16))
            value = value - part
        return jnp.concatenate([parts[left] for left, _ in terms], axis=1)

    gram = jnp.stack([stoich[p] * stoich[q] for p, q in pairs(NX)])
    cross = jnp.stack([stoich[:, i] * stoich[:, j] for i, j in pairs(NC)])
    return table(gram, ALL), table(cross, MOST), table(stoich.T, ALL)


def pairs(order):
    return [(i, j) for i in range(order) for j in range(i + 1)]


def solve_spd(matrix, rhs):
    order = len(rhs)
    lower, inverse, middle = {}, [], []
    for outer in range(order):
        scaled = {}
        for inner in range(outer):
            total = matrix(outer, inner)
            for other in range(inner):
                total = total - scaled[other] * lower[inner, other]
            scaled[inner] = total
            lower[outer, inner] = total * inverse[inner]
        total = matrix(outer, outer)
        value = rhs[outer]
        for other in range(outer):
            total = total - scaled[other] * lower[outer, other]
            value = value - lower[outer, other] * middle[other]
        inverse.append(1.0 / total)
        middle.append(value)
    result = [None] * order
    for outer in reversed(range(order)):
        total = middle[outer] * inverse[outer]
        for other in range(outer + 1, order):
            total = total - lower[other, outer] * result[other]
        result[outer] = total
    return result


def entries(value, diagonal):
    order = len(diagonal)
    at = {pair: SUB * k for k, pair in enumerate(pairs(order))}

    def entry(i, j):
        part = value[at[i, j] : at[i, j] + SUB]
        return part + diagonal[i] if i == j else part

    return entry


def speciate(totals, stoich, logk, gram, cross, back):
    def log_complexes(logfree):
        out = []
        for p in range(NX):
            total = logk(p)
            for i in range(NC):
                total = total + stoich(p, i) * logfree[i]
            out.append(total)
        return out

    def spread(parts):
        taken = dot(back, stack(parts, ALL))
        return [taken[SUB * i : SUB * (i + 1)] for i in range(NC)]

    logfree = [jnp.log(t) for t in totals]
    invfree = [1.0 / t for t in totals]
    weights = dot(gram, stack(split(jnp.concatenate(invfree, axis=0), 3), ALL))
    inverse = [jnp.exp(-jnp.maximum(v, -80.0)) for v in log_complexes(logfree)]
    bound = solve_spd(entries(weights, inverse), [jnp.ones_like(totals[0])] * NX)
    taken = spread(split(jnp.concatenate(bound, axis=0), 3))
    logfree = [x - b * v for x, b, v in zip(logfree, taken, invfree)]
    for sweep in range(ITERS - 1):
        free = [jnp.exp(x) for x in logfree]
        complexes = [jnp.exp(v) for v in log_complexes(logfree)]
        parts = split(jnp.concatenate(complexes, axis=0), 3)
        jacobian = entries(dot(cross, stack(parts, MOST)), free)
        excess = [(t - f) - b for t, f, b in zip(totals, free, spread(parts))]
        logfree = [x + d for x, d in zip(logfree, solve_spd(jacobian, excess))]
    return [jnp.exp(x) for x in logfree] + [jnp.exp(v) for v in log_complexes(logfree)]


def react_kernel(
    recv_ref, lanes_ref, message_ref, gram_ref, cross_ref, back_ref, stoich_ref, logk_ref,
    out_ref, coef, carry, rows_buf,
):
    lane = lax.broadcasted_iota(jnp.int32, (SUB, WIN), 1)
    row = lax.broadcasted_iota(jnp.int32, (SUB, WIN), 0)
    cell = lax.broadcasted_iota(jnp.int32, (WIN, WIN), 0)
    odd = lane >= HALF
    for p in range(NX):
        for i in range(NC):
            coef[p * NC + i] = jnp.full((SUB, WIN), stoich_ref[p, i], F32)
        coef[NX * NC + p] = jnp.full((SUB, WIN), logk_ref[p], F32)
    for c in range(NC):
        carry[c] = jnp.broadcast_to(message_ref[pl.ds(256 + c, 1), :], (SUB, WIN))
    rows_buf[...] = jnp.zeros(rows_buf.shape, F32)
    for b in range(BATCH):
        rows_buf[pl.ds(b * SUB * PAD + NQ - 1, SUB, stride=PAD), :] = jnp.ones((SUB, WIN), F32)

    def swap(value):
        return pltpu.roll(value, HALF, 1)

    def wide(value):
        return jnp.concatenate([value] * BATCH, axis=1)

    def step(index, unused):
        moved = [[] for _ in range(NC)]
        places = []
        for b in range(BATCH):
            source = index * BATCH + b
            base = pl.multiple_of(source * SUB, SUB)
            slot = message_ref[pl.ds(base, SUB), :].astype(jnp.int32)
            local = jnp.take_along_axis(lanes_ref[source], slot, axis=1).astype(jnp.int32)
            places.append(local)
            courant = message_ref[pl.ds(base + WIN, SUB), :]
            ratio = 1.0 / (1.0 + courant)
            weight = courant * ratio
            pair = jnp.where(odd, weight * swap(weight), weight)
            run = jnp.where(odd, pair, swap(pair))
            factors = []
            for reach in (1, 2, 4):
                factors.append(jnp.where(row >= reach, run, 0.0))
                run = run * jnp.where(row >= reach, pltpu.roll(run, reach, 0), 1.0)
            for c in range(NC):
                part = jnp.take_along_axis(recv_ref[source, c], local, axis=1) * ratio
                part = jnp.where(odd, weight * swap(part) + part, part)
                total = jnp.where(odd, part, swap(part))
                for level, reach in enumerate((1, 2, 4)):
                    total = total + factors[level] * pltpu.roll(total, reach, 0)
                before = carry[c]
                total = total + run * before
                carry[c] = jnp.broadcast_to(total[SUB - 1 :, :], (SUB, WIN))
                ahead = jnp.where(row == 0, before, pltpu.roll(total, 1, 0))
                moved[c].append(part + pair * ahead)
        species = speciate(
            [jnp.concatenate(parts, axis=1) for parts in moved],
            lambda p, i: wide(coef[p * NC + i]),
            lambda p: wide(coef[NX * NC + p]),
            gram_ref[...],
            cross_ref[...],
            back_ref[...],
        )
        for q in range(NC + NX):
            for b in range(BATCH):
                rows_buf[pl.ds(b * SUB * PAD + q, SUB, stride=PAD), :] = species[q][
                    :, b * WIN : (b + 1) * WIN
                ]
        for b in range(BATCH):
            for kt in range(SUB):
                hot = (cell == jnp.broadcast_to(places[b][kt : kt + 1, :], (WIN, WIN))).astype(BF16)
                value = rows_buf[pl.ds((b * SUB + kt) * PAD, PAD), :]
                both = lax.dot_general(
                    jnp.concatenate(split(value, 2), axis=0),
                    hot,
                    (((1,), (1,)), ((), ())),
                    preferred_element_type=F32,
                )
                sums = both[:PAD] + both[PAD:]
                out_ref[index * BATCH + b, pl.ds(kt, NQ, stride=SUB), :] = sums[:NQ]
        return unused

    lax.fori_loop(0, FLOW // BATCH, step, 0)


def react(recv, lanes, message, stoich, logk):
    return pl.pallas_call(
        react_kernel,
        out_shape=jax.ShapeDtypeStruct((FLOW, NQ * SUB, WIN), F32),
        in_specs=[pl.BlockSpec(memory_space=pltpu.VMEM)] * 6
        + [pl.BlockSpec(memory_space=pltpu.SMEM)] * 2,
        scratch_shapes=[
            pltpu.VMEM((NX * NC + NX, SUB, WIN), F32),
            pltpu.VMEM((NC, SUB, WIN), F32),
            pltpu.VMEM((BATCH * SUB * PAD, WIN), F32),
        ],
        compiler_params=pltpu.CompilerParams(vmem_limit_bytes=32 * 1024 * 1024),
        name="react",
    )(recv, lanes, message, *tables(stoich), stoich, logk)


def body(cell_state, inflow, courant, pick, node_slot, stoich, logk):
    block = SIDE * SUB * WIN
    column = lax.axis_index("h") * SIDE + lax.axis_index("q")
    mine = lax.dynamic_slice_in_dim(cell_state, column * block, block, 1)
    mine = jnp.transpose(mine.reshape(NC, SIDE, SUB, WIN), (1, 0, 2, 3))
    send = jnp.broadcast_to(mine[None], (SIDE, SIDE, NC, SUB, WIN)).reshape(FLOW, NC, SUB, WIN)
    recv = lax.all_to_all(send, ("z", "y"), 0, 0, tiled=True)
    start = jnp.concatenate([inflow, inflow], axis=1)
    start = jnp.concatenate([start, start[:4]], axis=0)
    low = WIN - 1
    message = jnp.concatenate(
        [
            jnp.bitwise_and(node_slot, low).astype(F32).reshape(WIN, WIN),
            courant.reshape(WIN, WIN),
            start,
            jnp.bitwise_and(pick, low).astype(F32).reshape(WIN, WIN),
        ],
        axis=0,
    )
    route = []
    for z in range(SIDE):
        for y in range(SIDE):
            for x in range(SIDE):
                for h in range(2):
                    source = (z * SIDE + y) * 2 * SIDE + x * 2 + h
                    route.append((source, (x * SIDE + y) * 2 * SIDE + h * SIDE + z))
    message = lax.ppermute(message, ("z", "y", "h", "q"), route)
    recv, message = lax.optimization_barrier((recv, message))
    lanes = message[2 * WIN + FLOW :].reshape(FLOW, SUB, WIN)
    lanes = lax.all_to_all(lanes, ("q", "y"), 0, 0, tiled=True)
    sums = react(recv, lanes, message[: 2 * WIN + FLOW], stoich, logk)
    back = lax.all_to_all(sums, ("z", "y"), 0, 0, tiled=True)
    back = jnp.sum(back.reshape(SIDE, SIDE, NQ, SUB * WIN), axis=0)
    means = back[:, : NQ - 1] / jnp.maximum(back[:, NQ - 1 :], 1.0)
    return jnp.transpose(means, (1, 0, 2)).reshape(NQ - 1, block)


def solution(mesh):
    grid = Mesh(mesh.devices.reshape(SIDE, SIDE, 2, SIDE), ("z", "y", "h", "q"))
    flow, group = ("z", "y"), ("h", "q")
    every = P(None, flow + group)
    placed = (P(None, flow), every, every, P(group, flow, None, None), every, P(), P())
    return jax.shard_map(body, mesh=grid, in_specs=placed, out_specs=every, check_vma=False)
```

time: 402 us -> 99.9 us (0.25); the launches traced: 394 us -> 98.8 us
  other arithmetic: 118 us -> 10.7 us
  waiting for transfers between devices: 107 us -> 0.65 us
  matrix products: 81.8 us -> 0 us
  local copies, waits for them, and re-layouts: 56 us -> 27.4 us
  blocking collectives: 0 us -> 25.7 us
  Pallas kernels: 0 us -> 16 us
  between operations: 15.4 us -> 0.27 us
    mul x26 -> x13, other arithmetic: 98.6 us -> 4.63 us  [the longest x3 2.75 us: table(): value = small[:, None, :, None] * eye[None, :, None, :]]
    dot_general x17 -> x0, matrix products: 81.8 us -> none  [the longest x4 51.5 us: speciate(): jnp.einsum('pi,pj,pn->ijn', stoich, stoich, complexes, precision=lax.Prec...]
    psum x1 -> x0, waiting for transfers between devices: 67.4 us -> none  [body(): full_sums, full_counts = lax.psum((cell_sums, cell_counts), 'group')]
    all_to_all x3 -> x2, waiting for transfers between devices: 39.2 us -> 0.65 us  [the longest x1 0.64 us: body(): lanes = lax.all_to_all(lanes, ('q', 'y'), 0, 0, tiled=True)]
    all_to_all x0 -> x1, blocking collectives: none -> 25.7 us  [body(): back = lax.all_to_all(sums, ('z', 'y'), 0, 0, tiled=True)]
    pallas_call x0 -> x1, Pallas kernels: none -> 16 us  [react(): pl.pallas_call(react_kernel, out_shape=jax.ShapeDtypeStruct((FLOW, NQ * S...]
    pad x28 -> x0, local copies, waits for them, and re-layouts: 12.6 us -> none  [body(): lax.associative_scan(compose_nodes, (weight, source), axis=0)]
    another operation x4 -> x3, local copies, waits for them, and re-layouts: 14.8 us -> 2.34 us  [the longest x2 2.19 us: tables(): gram = jnp.stack([stoich[p] * stoich[q] for p, q in pairs(NX)])]
  transfers between devices with their start and end apart: 4 -> 3, of which waited for: 4 -> 1; matrix products, arithmetic and copies ran while one was open for 2% -> 28% of each run, Pallas kernels for 0% -> 0%
where the time goes in v1:
time: 99.9 us; the launch traced here: 98.8 us
  local copies, waits for them, and re-layouts  27.4 us (27%)
  blocking collectives  25.7 us (26%)
  starting transfers between devices  18.1 us (18%)
  Pallas kernels  16 us (16%)
  other arithmetic  10.7 us (11%)
    all_to_all x1, blocking collectives, body(): back = lax.all_to_all(sums, ('z', 'y'), 0, 0, tiled=True)  25.7 us
    pallas_call x1, Pallas kernels, react(): pl.pallas_call(react_kernel, out_shape=jax.ShapeDtypeStruct((FLOW, NQ * S...  16 us
    all_to_all x1, starting transfers between devices, body(): recv = lax.all_to_all(send, ('z', 'y'), 0, 0, tiled=True)  8.26 us
    mul x6, local copies, waits for them, and re-layouts, table(): value = small[:, None, :, None] * eye[None, :, None, :]  6.5 us
    all_to_all x1, starting transfers between devices, body(): lanes = lax.all_to_all(lanes, ('q', 'y'), 0, 0, tiled=True)  6.39 us
    convert_element_type x3, other arithmetic, table(): parts.append(part.astype(BF16))  4.2 us
    concatenate x1, local copies, waits for them, and re-layouts, body(): jnp.concatenate([jnp.bitwise_and(node_slot, low).astype(F32).reshape(WIN,...  3.75 us
    unnamed x23, local copies, waits for them, and re-layouts  3.73 us
  transfers between devices with their start and end apart: 3, of which 1 were waited for; matrix products, arithmetic and copies ran while one was open for 28% of the time, Pallas kernels for 0%

profile of v1, /device:TPU:0, one launch (start us, length us, event | category | flops | bytes accessed | tf_op | source)
XLA Modules:
  0.0 98.8 jit_solution(3664804154052476317)
XLA Ops:
  0.0 0.0 copy-start
  0.0 1.6 %copy-done = f32[12,32768]{1,0:T(8,128)S(1)} copy-done((f32[12,32768]{1,0:T(8,128)S(1)}, f32[12,32768]{1,0:T(8,128)}, u32[]{:S(2)}) %copy-start) | copy-done | bytes 1572888
  1.6 0.1 copy.291
  1.7 0.0 copy-start.8
  1.7 0.0 copy-start.6
  1.7 0.0 copy-start.5
  1.8 0.0 copy-start.7
  1.8 1.0 broadcast_in_dim.2
  2.7 8.3 %all-to-all-start = ((f32[16,12,8,128]{3,2,1,0:T(8,128)}), f32[16,12,8,128]{3,2,1,0:T(8,128)S(1)}, u32[]{:S(2)}, u32[]{:S(2)}) async-start(f32[16,12,8,128]{3,2,1,0:T(8,128)} %bitcast.184), calls=%async_computation | async-start | bytes 1572864 | tf_op jit(solution)/shard_map/all_to_all | solution.py:243
  11.0 0.0 copy-done.8
  11.0 0.1 pad_maximum_fusion
  11.1 0.1 fusion.6
  11.2 0.1 copy.200
  11.3 0.1 reshape.1370
  11.4 0.1 copy.201
  11.5 0.1 reshape.1371
  11.6 3.7 %concatenate.16 = f32[400,128]{1,0:T(8,128)} concatenate(f32[128,128]{1,0:T(8,128)S(1)} %reshape.1370, f32[128,128]{1,0:T(8,128)S(1)} %reshape.1371, f32[12,128]{1,0:T(8,128)S(1)} %pad_maximum_fusion, f32[4,128]{1,0:T(4,128)S(1)} %fusion.6, f32[128,128]{1,0:T(8,128)S(1)} %reshape.1372), dimensions={0} | concatenate | bytes 409600 | tf_op jit(solution)/shard_map/concatenate | solution.py:247
  15.4 3.4 %collective-permute-start = (f32[400,128]{1,0:T(8,128)}, f32[400,128]{1,0:T(8,128)}, u32[]{:S(2)}, u32[]{:S(2)}) collective-permute-start(f32[400,128]{1,0:T(8,128)} %concatenate.16), channel_id=1, source_target_pairs={{0,0},{1,4},{2,32},{3,36},{4,64},{5,68},{6,96},{7,100},{8,8},{9,12... | collective-permute-start | bytes 614408 | tf_op jit(solution)/shard_map/ppermute | solution.py:263
  18.8 0.1 multiply_bitcast_fusion
  18.9 0.1 multiply_bitcast_fusion.2
  18.9 0.1 multiply_bitcast_fusion.1
  19.0 0.1 multiply_bitcast_fusion.3
  19.1 0.1 multiply_bitcast_fusion.4
  19.2 0.1 multiply_bitcast_fusion.5
  19.3 0.1 multiply_bitcast_fusion.6
  19.4 0.1 multiply_bitcast_fusion.56
  19.4 0.6 slice_multiply_fusion
  20.1 0.1 stack.5
  20.2 1.5 %broadcast_multiply_fusion = f32[78,8,6,8]{1,0,3,2:T(8,128)} fusion(f32[8,8]{0,1:T(8,128)S(1)} %fusion.5, f32[78,6]{0,1:T(8,128)S(1)} %stack.5), kind=kLoop, calls=%fused_computation | loop fusion | flops 29952 | bytes 121936 | tf_op jit(solution)/shard_map/mul | solution.py:51
  21.7 0.1 broadcast_multiply_fusion.2
  21.8 0.6 slice_multiply_fusion.1
  22.4 2.4 %mul.1341 = f32[624,48]{0,1:T(8,128)S(1)} reshape(f32[78,8,6,8]{1,0,3,2:T(8,128)} %broadcast_multiply_fusion) | data formatting | bytes 239616 | tf_op jit(solution)/shard_map/mul | solution.py:51
  24.9 0.9 copy.284
  25.7 0.2 mul.1345
  25.9 0.7 copy.287
  26.6 0.9 copy.283
  27.5 2.1 %stack.4 = f32[21,12]{1,0:T(8,128)S(1)} concatenate(f32[1,12]{1,0:T(1,128)} %get-tuple-element.115, f32[1,12]{1,0:T(1,128)} %get-tuple-element.114, f32[1,12]{1,0:T(1,128)S(1)} %get-tuple-element.96, f32[1,12]{1,0:T(1,128)} %get-tuple-element.113, f32[1,12]{1,0:T(1,128)S(1)} %get-tuple-element.97, f32[1,12]{1,0:T(1,128)S(1)} %get-tuple-element.98, f32[1,12]{1,0:T(1,128)} %get-tuple-element.112, ...), dimensions={0} | concatenate | bytes 2016 | tf_op jit(solution)/shard_map/stack | solution.py:60
  29.6 0.1 copy.202
  29.7 1.2 %broadcast_multiply_fusion.1 = f32[21,8,12,8]{1,0,3,2:T(8,128)} fusion(f32[8,8]{0,1:T(8,128)S(1)} %fusion.5, f32[21,12]{0,1:T(8,128)S(1)} %copy.202), kind=kLoop, calls=%fused_computation.1 | loop fusion | flops 16128 | bytes 65776 | tf_op jit(solution)/shard_map/mul | solution.py:51
  30.9 1.6 %mul.1181 = f32[168,96]{0,1:T(8,128)S(1)} reshape(f32[21,8,12,8]{1,0,3,2:T(8,128)} %broadcast_multiply_fusion.1) | data formatting | bytes 129024 | tf_op jit(solution)/shard_map/mul | solution.py:51
  32.5 0.7 copy.203
  33.2 0.7 copy.286
  33.9 1.2 %reduce-precision_convert_fusion = (bf16[624,48]{1,0:T(8,128)(2,1)S(1)}, bf16[624,48]{1,0:T(8,128)(2,1)S(1)}) fusion(f32[624,48]{1,0:T(8,128)S(1)} %copy-done.4, f32[624,48]{1,0:T(8,128)} %copy.283), kind=kLoop, calls=%fused_computation.4 | loop fusion | flops 119808 | bytes 359424 | tf_op jit(solution)/shard_map/convert_element_type | solution.py:56
  35.1 0.0 copy-start.3
  35.1 1.6 %fusion.2 = (bf16[168,96]{1,0:T(8,128)(2,1)}, bf16[168,96]{1,0:T(8,128)(2,1)}, bf16[168,96]{1,0:T(8,128)(2,1)}) fusion(f32[168,96]{1,0:T(8,128)} %copy.203), kind=kLoop, calls=%fused_computation.12 | loop fusion | flops 129024 | bytes 161280 | tf_op jit(solution)/shard_map/convert_element_type | solution.py:56
  36.6 0.0 collective-permute-done
  36.6 0.0 all-to-all-done.recv_ref
  36.6 1.5 %slice_bitcast_fusion = f32[16,8,128]{2,1,0:T(8,128)} fusion(f32[400,128]{1,0:T(8,128)} %collective-permute-done), kind=kLoop, calls=%fused_computation.15 | loop fusion | bytes 131072 | tf_op jit(solution)/shard_map/reshape | solution.py:265
  38.1 6.4 %all-to-all-start.1 = ((f32[16,8,128]{2,1,0:T(8,128)}), f32[16,8,128]{2,1,0:T(8,128)}, u32[]{:S(2)}, u32[]{:S(2)}) async-start(f32[16,8,128]{2,1,0:T(8,128)} %slice_bitcast_fusion), calls=%async_computation.1 | async-start | bytes 131072 | tf_op jit(solution)/shard_map/all_to_all | solution.py:266
  44.5 1.5 %fusion.4 = (bf16[96,48]{1,0:T(8,128)(2,1)}, bf16[96,48]{1,0:T(8,128)(2,1)}, bf16[96,48]{1,0:T(8,128)(2,1)S(1)}) fusion(f32[96,48]{1,0:T(8,128)} %copy.287, f32[96,48]{1,0:T(8,128)} %copy.286), kind=kLoop, calls=%fused_computation.19 | loop fusion | flops 32256 | bytes 64512 | tf_op jit(solution)/shard_map/convert_element_type | solution.py:56
  46.0 0.4 concatenate.18.cross_ref
  46.5 1.1 %concatenate.17.gram_ref = bf16[168,576]{1,0:T(8,128)(2,1)S(1)} concatenate(bf16[168,96]{1,0:T(8,128)(2,1)} %get-tuple-element.15, bf16[168,96]{1,0:T(8,128)(2,1)} %get-tuple-element.15, bf16[168,96]{1,0:T(8,128)(2,1)} %get-tuple-element.15, bf16[168,96]{1,0:T(8,128)(2,1)} %get-tuple-element.14, bf16[168,96]{1,0:T(8,128)(2,1)} %get-tuple-element.14, ...), dimensions={1} | concatenate | bytes 387072 | tf_op jit(solution)/shard_map/concatenate | solution.py:58
  47.5 0.9 concatenate.19.back_ref
  48.5 1.6 %slice.48.message_ref = f32[272,128]{1,0:T(8,128)} slice(f32[400,128]{1,0:T(8,128)} %collective-permute-done), slice={[0:272], [0:128]} | slice | bytes 278528 | tf_op jit(solution)/shard_map/slice | solution.py:267
  50.0 0.6 all-to-all-done.1.lanes_ref
  50.7 0.0 copy-done.3
  50.7 0.9 copy-done.2
  51.6 16.0 %react.1 = f32[16,152,128]{2,1,0:T(8,128)S(1)} custom-call(f32[16,12,8,128]{3,2,1,0:T(8,128)S(1)} %all-to-all-done.recv_ref, f32[16,8,128]{2,1,0:T(8,128)} %all-to-all-done.1.lanes_ref, f32[272,128]{1,0:T(8,128)S(1)} %copy-done.2, bf16[168,576]{1,0:T(8,128)(2,1)S(1)} %concatenate.17.gram_ref, bf16[624,240]{1,0:T(8,128)(2,1)S(1)} %concatenate.18.cross_ref, ...), custom_call_target="tpu_custom_call" | custom-call | tf_op jit(solution)/shard_map/react/pallas_call | solution.py:222
  67.7 25.7 %all_to_all.15 = f32[16,152,128]{2,1,0:T(8,128)} all-to-all(f32[16,152,128]{2,1,0:T(8,128)S(1)} %react.1), channel_id=1, replica_groups=mesh['z'=4,'y'=4,'h'=2,'q'=4] {'z','y'}, dimensions={0} | all-to-all | bytes 2490368 | tf_op jit(solution)/shard_map/all_to_all | solution.py:268
  93.4 2.5 %reshape.1374 = f32[4,4,19,1024]{3,2,1,0:T(8,128)} reshape(f32[16,152,128]{2,1,0:T(8,128)} %all_to_all.15) | data formatting | bytes 2490368 | tf_op jit(solution)/shard_map/reshape | solution.py:269
  95.9 1.6 %reduce_sum.9 = f32[4,19,1024]{2,1,0:T(8,128)S(1)} reduce(f32[4,4,19,1024]{3,2,1,0:T(8,128)} %reshape.1374, f32[]{:T(128)} %constant.22.clone.1), dimensions={0}, to_apply=%region_0.0 | reduce | flops 233472 | bytes 1556484 | tf_op jit(solution)/shard_map/reduce_sum | solution.py:269
  97.5 0.2 copy.289
  97.7 0.1 pad.2
  97.8 1.0 copy.292
  (20 shorter events, 0.2 us)
Async XLA Ops:
  0.0 1.6 %copy-start = (f32[12,32768]{1,0:T(8,128)S(1)}, f32[12,32768]{1,0:T(8,128)}, u32[]{:S(2)}) copy-start(f32[12,32768]{1,0:T(8,128)} %param.7) | copy-start | bytes 4718596
  1.7 9.3 %copy-start.8 = (f32[12,64]{1,0:T(8,128)S(1)}, f32[12,64]{1,0:T(8,128)}, u32[]{:S(2)}) copy-start(f32[12,64]{1,0:T(8,128)} %param.8) | copy-start | bytes 9220
  1.7 9.5 %copy-start.6 = (s32[256,64]{0,1:T(8,128)S(1)}, s32[256,64]{0,1:T(8,128)}, u32[]{:S(2)}) copy-start(s32[256,64]{0,1:T(8,128)} %param.11) | copy-start | bytes 196612
  1.7 9.6 %copy-start.5 = (f32[256,64]{0,1:T(8,128)S(1)}, f32[256,64]{0,1:T(8,128)}, u32[]{:S(2)}) copy-start(f32[256,64]{0,1:T(8,128)} %param.9) | copy-start | bytes 196612
  1.8 9.8 %copy-start.7 = (s32[1,1,16,1024]{3,2,1,0:T(8,128)S(1)}, s32[1,1,16,1024]{3,2,1,0:T(8,128)}, u32[]{:S(2)}) copy-start(s32[1,1,16,1024]{3,2,1,0:T(8,128)} %param.10) | copy-start | bytes 196612
  2.7 16.1 %copy-start.1 = (f32[6,12]{1,0:T(8,128)S(1)}, f32[6,12]{1,0:T(8,128)}, u32[]{:S(2)}) copy-start(f32[6,12]{1,0:T(8,128)} %stoich_ref.1) | copy-start | bytes 868
  2.7 33.9 %all-to-all-start = ((f32[16,12,8,128]{3,2,1,0:T(8,128)}), f32[16,12,8,128]{3,2,1,0:T(8,128)S(1)}, u32[]{:S(2)}, u32[]{:S(2)}) async-start(f32[16,12,8,128]{3,2,1,0:T(8,128)} %bitcast.184), calls=%async_computation | async-start | bytes 1572864 | tf_op jit(solution)/shard_map/all_to_all | solution.py:243
  15.4 21.3 %collective-permute-start = (f32[400,128]{1,0:T(8,128)}, f32[400,128]{1,0:T(8,128)}, u32[]{:S(2)}, u32[]{:S(2)}) collective-permute-start(f32[400,128]{1,0:T(8,128)} %concatenate.16), channel_id=1, source_target_pairs={{0,0},{1,4},{2,32},{3,36},{4,64},{5,68},{6,96},{7,100},{8,8},{9,12... | collective-permute-start | bytes 614408 | tf_op jit(solution)/shard_map/ppermute | solution.py:263
  26.6 7.3 %copy-start.4 = (f32[624,48]{1,0:T(8,128)S(1)}, f32[624,48]{1,0:T(8,128)}, u32[]{:S(2)}) copy-start(f32[624,48]{1,0:T(8,128)} %copy.284) | copy-start | bytes 359428
  35.1 15.6 %copy-start.3 = (f32[6]{0:T(128)S(1)}, f32[6]{0:T(128)}, u32[]{:S(2)}) copy-start(f32[6]{0:T(128)} %logk_ref.1) | copy-start | bytes 76
  38.1 12.6 %all-to-all-start.1 = ((f32[16,8,128]{2,1,0:T(8,128)}), f32[16,8,128]{2,1,0:T(8,128)}, u32[]{:S(2)}, u32[]{:S(2)}) async-start(f32[16,8,128]{2,1,0:T(8,128)} %slice_bitcast_fusion), calls=%async_computation.1 | async-start | bytes 131072 | tf_op jit(solution)/shard_map/all_to_all | solution.py:266
  50.7 0.9 copy-start.2

commit v2 on v1

--- a/solution.py
+++ b/solution.py
@@ -17,6 +17,7 @@
 FLOW = 16
 SUB = 8
 HALF = 64
+LANES = 2 * WIN + FLOW
 BATCH = 8
 BF16 = jnp.bfloat16
 F32 = jnp.float32
@@ -43,23 +44,105 @@
     return jnp.concatenate([parts[right] for _, right in terms], axis=0)
 
 
-def tables(stoich):
-    eye = jnp.eye(SUB, dtype=F32)
-
-    def table(small, terms):
-        rows, columns = small.shape
-        value = small[:, None, :, None] * eye[None, :, None, :]
-        value = value.reshape(rows * SUB, columns * SUB)
-        parts = []
-        for _ in range(3):
-            part = lax.reduce_precision(value, 8, 7)
-            parts.append(part.astype(BF16))
-            value = value - part
-        return jnp.concatenate([parts[left] for left, _ in terms], axis=1)
-
-    gram = jnp.stack([stoich[p] * stoich[q] for p, q in pairs(NX)])
-    cross = jnp.stack([stoich[:, i] * stoich[:, j] for i, j in pairs(NC)])
-    return table(gram, ALL), table(cross, MOST), table(stoich.T, ALL)
+def build_tables(stoich_ref, gram_ref, cross_ref, back_ref):
+    def spread(count, terms, pick):
+        lane = lax.broadcasted_iota(jnp.int32, (SUB, len(terms) * count * SUB), 1)
+        row = lax.broadcasted_iota(jnp.int32, lane.shape, 0)
+        which = lane % (count * SUB) // SUB
+        vectors = []
+        for outer in range(NC + NX - count):
+            value = jnp.zeros(lane.shape, F32)
+            for inner in range(count):
+                value = jnp.where(which == inner, pick(outer, inner), value)
+            vectors.append(value)
+        return vectors, lane // (count * SUB), lane % SUB == row
+
+    def write(ref, values, term, same, terms):
+        for at in range(0, len(values), 2):
+            value = jnp.concatenate([jnp.where(same, v, 0.0) for v in values[at : at + 2]], axis=0)
+            where = jnp.concatenate([term] * len(values[at : at + 2]), axis=0)
+            parts = split(value, 3)
+            out = parts[0].astype(F32)
+            for k, (left, _) in enumerate(terms):
+                if left:
+                    out = jnp.where(where == k, parts[left].astype(F32), out)
+            ref[pl.ds(SUB * at, out.shape[0]), :] = out.astype(BF16)
+
+    rows, term, same = spread(NC, ALL, lambda p, i: stoich_ref[p, i])
+    products = [rows[p] * rows[q] for p, q in pairs(NX)]
+    write(gram_ref, products + [jnp.zeros_like(products[0])], term, same, ALL)
+    rows, term, same = spread(NX, ALL, lambda i, p: stoich_ref[p, i])
+    write(back_ref, rows, term, same, ALL)
+    rows, term, same = spread(NX, MOST, lambda i, p: stoich_ref[p, i])
+    write(cross_ref, [rows[i] * rows[j] for i, j in pairs(NC)], term, same, MOST)
+
+
+def cells_kernel(column_ref, cell_ref, out_ref):
+    for y in range(SIDE):
+        for kt in range(SUB):
+            value = cell_ref[:, pl.ds((y * SUB + kt) * WIN, WIN)]
+            for z in range(SIDE):
+                out_ref[z * SIDE + y, pl.ds(kt, NC, stride=SUB), :] = value
+
+
+def cells_to_send(column, cell_state):
+    block = SIDE * SUB * WIN
+    return pl.pallas_call(
+        cells_kernel,
+        out_shape=jax.ShapeDtypeStruct((FLOW, NC * SUB, WIN), F32),
+        grid_spec=pltpu.PrefetchScalarGridSpec(
+            num_scalar_prefetch=1,
+            grid=(1,),
+            in_specs=[pl.BlockSpec((NC, block), lambda step, column: (0, column[0]))],
+            out_specs=pl.BlockSpec((FLOW, NC * SUB, WIN), lambda step, column: (0, 0, 0)),
+        ),
+        name="cells",
+    )(column, cell_state)
+
+
+def pack_kernel(slot_ref, courant_ref, inflow_ref, pick_ref, message_ref, first_buf, second_buf):
+    def rows(ref, buffer, value):
+        buffer[...] = jnp.transpose(value)
+        even = buffer[pl.ds(0, WIN, stride=2), :]
+        odd = buffer[pl.ds(1, WIN, stride=2), :]
+        ref[...] = jnp.concatenate([even, odd], axis=1)
+
+    low = jnp.bitwise_and(slot_ref[...], WIN - 1).astype(F32)
+    rows(message_ref.at[pl.ds(0, WIN)], first_buf, low)
+    rows(message_ref.at[pl.ds(WIN, WIN)], second_buf, courant_ref[...])
+    first = inflow_ref[...]
+    message_ref[pl.ds(2 * WIN, NC), :] = jnp.concatenate([first, first], axis=1)
+    message_ref[pl.ds(2 * WIN + NC, FLOW - NC), :] = jnp.zeros((FLOW - NC, WIN), F32)
+    for kt in range(SUB):
+        part = jnp.bitwise_and(pick_ref[0, 0, :, pl.ds(kt * WIN, WIN)], WIN - 1)
+        message_ref[pl.ds(LANES + kt, FLOW, stride=SUB), :] = part.astype(F32)
+
+
+def pack(node_slot, courant, inflow, pick):
+    return pl.pallas_call(
+        pack_kernel,
+        out_shape=jax.ShapeDtypeStruct((LANES + WIN, WIN), F32),
+        scratch_shapes=[pltpu.VMEM((2 * WIN, HALF), F32)] * 2,
+        name="pack",
+    )(node_slot.T, courant.T, inflow, pick)
+
+
+def mean_kernel(sums_ref, out_ref):
+    for y in range(SIDE):
+        for kt in range(SUB):
+            total = sums_ref[y, pl.ds(kt, NQ, stride=SUB), :]
+            for z in range(1, SIDE):
+                total = total + sums_ref[z * SIDE + y, pl.ds(kt, NQ, stride=SUB), :]
+            share = 1.0 / jnp.maximum(total[NQ - 1 :, :], 1.0)
+            out_ref[:, pl.ds((y * SUB + kt) * WIN, WIN)] = total[: NQ - 1] * share
+
+
+def mean(sums):
+    return pl.pallas_call(
+        mean_kernel,
+        out_shape=jax.ShapeDtypeStruct((NQ - 1, SIDE * SUB * WIN), F32),
+        name="mean",
+    )(sums)
 
 
 def pairs(order):
@@ -136,9 +219,10 @@
 
 
 def react_kernel(
-    recv_ref, lanes_ref, message_ref, gram_ref, cross_ref, back_ref, stoich_ref, logk_ref,
-    out_ref, coef, carry, rows_buf,
+    recv_ref, lanes_ref, message_ref, stoich_ref, logk_ref,
+    out_ref, coef, carry, rows_buf, gram_ref, cross_ref, back_ref,
 ):
+    build_tables(stoich_ref, gram_ref, cross_ref, back_ref)
     lane = lax.broadcasted_iota(jnp.int32, (SUB, WIN), 1)
     row = lax.broadcasted_iota(jnp.int32, (SUB, WIN), 0)
     cell = lax.broadcasted_iota(jnp.int32, (WIN, WIN), 0)
@@ -147,11 +231,11 @@
         for i in range(NC):
             coef[p * NC + i] = jnp.full((SUB, WIN), stoich_ref[p, i], F32)
         coef[NX * NC + p] = jnp.full((SUB, WIN), logk_ref[p], F32)
-    for c in range(NC):
-        carry[c] = jnp.broadcast_to(message_ref[pl.ds(256 + c, 1), :], (SUB, WIN))
     rows_buf[...] = jnp.zeros(rows_buf.shape, F32)
     for b in range(BATCH):
         rows_buf[pl.ds(b * SUB * PAD + NQ - 1, SUB, stride=PAD), :] = jnp.ones((SUB, WIN), F32)
+    for c in range(NC):
+        carry[c] = jnp.broadcast_to(message_ref[pl.ds(2 * WIN + c, 1), :], (SUB, WIN))
 
     def swap(value):
         return pltpu.roll(value, HALF, 1)
@@ -178,7 +262,7 @@
                 factors.append(jnp.where(row >= reach, run, 0.0))
                 run = run * jnp.where(row >= reach, pltpu.roll(run, reach, 0), 1.0)
             for c in range(NC):
-                part = jnp.take_along_axis(recv_ref[source, c], local, axis=1) * ratio
+                part = jnp.take_along_axis(recv_ref[source, pl.ds(SUB * c, SUB), :], local, axis=1) * ratio
                 part = jnp.where(odd, weight * swap(part) + part, part)
                 total = jnp.where(odd, part, swap(part))
                 for level, reach in enumerate((1, 2, 4)):
@@ -192,7 +276,7 @@
             [jnp.concatenate(parts, axis=1) for parts in moved],
             lambda p, i: wide(coef[p * NC + i]),
             lambda p: wide(coef[NX * NC + p]),
-            gram_ref[...],
+            gram_ref[:168],
             cross_ref[...],
             back_ref[...],
         )
@@ -222,37 +306,24 @@
     return pl.pallas_call(
         react_kernel,
         out_shape=jax.ShapeDtypeStruct((FLOW, NQ * SUB, WIN), F32),
-        in_specs=[pl.BlockSpec(memory_space=pltpu.VMEM)] * 6
+        in_specs=[pl.BlockSpec(memory_space=pltpu.VMEM)] * 3
         + [pl.BlockSpec(memory_space=pltpu.SMEM)] * 2,
         scratch_shapes=[
             pltpu.VMEM((NX * NC + NX, SUB, WIN), F32),
             pltpu.VMEM((NC, SUB, WIN), F32),
             pltpu.VMEM((BATCH * SUB * PAD, WIN), F32),
+            pltpu.VMEM((176, len(ALL) * NC * SUB), BF16),
+            pltpu.VMEM((624, len(MOST) * NX * SUB), BF16),
+            pltpu.VMEM((96, len(ALL) * NX * SUB), BF16),
         ],
-        compiler_params=pltpu.CompilerParams(vmem_limit_bytes=32 * 1024 * 1024),
+        compiler_params=pltpu.CompilerParams(vmem_limit_bytes=48 * 1024 * 1024),
         name="react",
-    )(recv, lanes, message, *tables(stoich), stoich, logk)
+    )(recv, lanes, message, stoich, logk)
 
 
 def body(cell_state, inflow, courant, pick, node_slot, stoich, logk):
-    block = SIDE * SUB * WIN
+    everywhere = ("z", "y", "h", "q")
     column = lax.axis_index("h") * SIDE + lax.axis_index("q")
-    mine = lax.dynamic_slice_in_dim(cell_state, column * block, block, 1)
-    mine = jnp.transpose(mine.reshape(NC, SIDE, SUB, WIN), (1, 0, 2, 3))
-    send = jnp.broadcast_to(mine[None], (SIDE, SIDE, NC, SUB, WIN)).reshape(FLOW, NC, SUB, WIN)
-    recv = lax.all_to_all(send, ("z", "y"), 0, 0, tiled=True)
-    start = jnp.concatenate([inflow, inflow], axis=1)
-    start = jnp.concatenate([start, start[:4]], axis=0)
-    low = WIN - 1
-    message = jnp.concatenate(
-        [
-            jnp.bitwise_and(node_slot, low).astype(F32).reshape(WIN, WIN),
-            courant.reshape(WIN, WIN),
-            start,
-            jnp.bitwise_and(pick, low).astype(F32).reshape(WIN, WIN),
-        ],
-        axis=0,
-    )
     route = []
     for z in range(SIDE):
         for y in range(SIDE):
@@ -260,15 +331,15 @@
                 for h in range(2):
                     source = (z * SIDE + y) * 2 * SIDE + x * 2 + h
                     route.append((source, (x * SIDE + y) * 2 * SIDE + h * SIDE + z))
-    message = lax.ppermute(message, ("z", "y", "h", "q"), route)
-    recv, message = lax.optimization_barrier((recv, message))
-    lanes = message[2 * WIN + FLOW :].reshape(FLOW, SUB, WIN)
+    send = cells_to_send(column[None], cell_state)
+    recv = lax.all_to_all(send, ("z", "y"), 0, 0, tiled=True)
+    message = lax.ppermute(pack(node_slot, courant, inflow, pick), everywhere, route)
+    lanes = message[LANES:].reshape(FLOW, SUB, WIN)
+    recv, lanes = lax.optimization_barrier((recv, lanes))
     lanes = lax.all_to_all(lanes, ("q", "y"), 0, 0, tiled=True)
-    sums = react(recv, lanes, message[: 2 * WIN + FLOW], stoich, logk)
+    sums = react(recv, lanes, message, stoich, logk)
     back = lax.all_to_all(sums, ("z", "y"), 0, 0, tiled=True)
-    back = jnp.sum(back.reshape(SIDE, SIDE, NQ, SUB * WIN), axis=0)
-    means = back[:, : NQ - 1] / jnp.maximum(back[:, NQ - 1 :], 1.0)
-    return jnp.transpose(means, (1, 0, 2)).reshape(NQ - 1, block)
+    return mean(back)
 
 
 def solution(mesh):

time: 99.9 us -> 80.7 us (0.81)
  local copies, waits for them, and re-layouts: 27.4 us -> 0.01 us
  blocking collectives: 25.7 us -> 37.4 us
  other arithmetic: 10.7 us -> 0 us
  waiting for transfers between devices: 0.65 us -> 11.1 us
  starting transfers between devices: 18.1 us -> 9.84 us
  Pallas kernels: 16 us -> 21.7 us
    all_to_all x0 -> x1, blocking collectives: none -> 14.3 us  [body(): lanes = lax.all_to_all(lanes, ('q', 'y'), 0, 0, tiled=True)]
    all_to_all x1, waiting for transfers between devices: 0.01 us -> 11.1 us  [body(): recv = lax.all_to_all(send, ('z', 'y'), 0, 0, tiled=True)]
    mul x6 -> x0, local copies, waits for them, and re-layouts: 6.5 us -> none  [table(): value = small[:, None, :, None] * eye[None, :, None, :]]
    all_to_all x1 -> x0, starting transfers between devices: 6.39 us -> none  [body(): lanes = lax.all_to_all(lanes, ('q', 'y'), 0, 0, tiled=True)]
    concatenate x4 -> x0, local copies, waits for them, and re-layouts: 6.2 us -> none  [the longest x1 3.75 us: body(): jnp.concatenate([jnp.bitwise_and(node_slot, low).astype(F32).reshape(WIN,...]
    pallas_call x0 -> x3, Pallas kernels: none -> 6.08 us  [the longest x1 2.25 us: mean(): pl.pallas_call(mean_kernel, out_shape=jax.ShapeDtypeStruct((NQ - 1, SIDE...]
    mul x13 -> x0, other arithmetic: 4.63 us -> none  [the longest x3 2.75 us: table(): value = small[:, None, :, None] * eye[None, :, None, :]]
    convert_element_type x6 -> x0, other arithmetic: 4.22 us -> none  [the longest x3 4.2 us: table(): parts.append(part.astype(BF16))]
  transfers between devices with their start and end apart: 3 -> 2, of which waited for: 1 -> 1; matrix products, arithmetic and copies ran while one was open for 28% -> 0% of each run, Pallas kernels for 0% -> 2%
where the time goes in v2:
time: 80.7 us; the launch traced here: 80.1 us
  blocking collectives  37.4 us (46%)
  Pallas kernels  21.7 us (27%)
  waiting for transfers between devices  11.1 us (14%)
  starting transfers between devices  9.84 us (12%)
    all_to_all x1, blocking collectives, body(): back = lax.all_to_all(sums, ('z', 'y'), 0, 0, tiled=True)  23.2 us
    pallas_call x1, Pallas kernels, react(): pl.pallas_call(react_kernel, out_shape=jax.ShapeDtypeStruct((FLOW, NQ * S...  15.6 us
    all_to_all x1, blocking collectives, body(): lanes = lax.all_to_all(lanes, ('q', 'y'), 0, 0, tiled=True)  14.3 us
    all_to_all x1, waiting for transfers between devices, body(): recv = lax.all_to_all(send, ('z', 'y'), 0, 0, tiled=True)  11.1 us
    all_to_all x1, starting transfers between devices, body(): recv = lax.all_to_all(send, ('z', 'y'), 0, 0, tiled=True)  8.26 us
    pallas_call x1, Pallas kernels, mean(): pl.pallas_call(mean_kernel, out_shape=jax.ShapeDtypeStruct((NQ - 1, SIDE...  2.25 us
    pallas_call x1, Pallas kernels, cells_to_send(): pl.pallas_call(cells_kernel, out_shape=jax.ShapeDtypeStruct((FLOW, NC * S...  1.99 us
    pallas_call x1, Pallas kernels, pack(): pl.pallas_call(pack_kernel, out_shape=jax.ShapeDtypeStruct((LANES + WIN,...  1.85 us
  transfers between devices with their start and end apart: 2, of which 1 were waited for; matrix products, arithmetic and copies ran while one was open for 0% of the time, Pallas kernels for 2%

profile of v2, /device:TPU:0, one launch (start us, length us, event | category | flops | bytes accessed | tf_op | source)
XLA Modules:
  0.0 80.1 jit_solution(3524239174623173122)
XLA Ops:
  0.0 2.0 %cells.1 = f32[16,96,128]{2,1,0:T(8,128)} custom-call(s32[1]{0:T(128)} %bitcast.column_ref, f32[12,32768]{1,0:T(8,128)} %cell_ref.1), custom_call_target="tpu_custom_call" | custom-call | tf_op jit(solution)/shard_map/cells/pallas_call | solution.py:90
  2.0 0.0 copy-start
  2.0 0.0 copy-start.1
  2.0 8.3 %all-to-all-start = ((f32[16,96,128]{2,1,0:T(8,128)}), f32[16,96,128]{2,1,0:T(8,128)S(1)}, u32[]{:S(2)}, u32[]{:S(2)}) async-start(f32[16,96,128]{2,1,0:T(8,128)} %cells.1), calls=%async_computation | async-start | bytes 1572864 | tf_op jit(solution)/shard_map/all_to_all | solution.py:335
  10.3 1.9 %pack.1 = f32[400,128]{1,0:T(8,128)} custom-call(s32[64,256]{1,0:T(8,128)} %bitcast.5, f32[64,256]{1,0:T(8,128)} %bitcast.6, f32[12,64]{1,0:T(8,128)} %inflow_ref.1, s32[1,1,16,1024]{3,2,1,0:T(8,128)} %pick_ref.1), custom_call_target="tpu_custom_call" | custom-call | tf_op jit(solution)/shard_map/pack/pallas_call | solution.py:122
  12.1 1.6 %collective-permute-start = (f32[400,128]{1,0:T(8,128)}, f32[400,128]{1,0:T(8,128)S(1)}, u32[]{:S(2)}, u32[]{:S(2)}) collective-permute-start(f32[400,128]{1,0:T(8,128)} %pack.1), channel_id=1, source_target_pairs={{0,0},{1,4},{2,32},{3,36},{4,64},{5,68},{6,96},{7,100},{8,8},{9,12... | collective-permute-start | bytes 614408 | tf_op jit(solution)/shard_map/ppermute | solution.py:336
  13.7 0.0 collective-permute-done.message_ref
  13.7 11.1 %all-to-all-done.recv_ref = f32[16,96,128]{2,1,0:T(8,128)S(1)} async-done(((f32[16,96,128]{2,1,0:T(8,128)}), f32[16,96,128]{2,1,0:T(8,128)S(1)}, u32[]{:S(2)}, u32[]{:S(2)}) %all-to-all-start) | async-done | bytes 786464 | tf_op jit(solution)/shard_map/all_to_all | solution.py:335
  24.8 14.3 %all_to_all.15.lanes_ref = f32[16,8,128]{2,1,0:T(8,128)S(1)} all-to-all(f32[16,8,128]{2,1,0:T(8,128)S(1)} %slice_bitcast_fusion), channel_id=1, replica_groups=mesh['z'=4,'y'=4,'h'=2,'q'=4] {'q','y'}, dimensions={0} | all-to-all | bytes 131072 | tf_op jit(solution)/shard_map/all_to_all | solution.py:339
  39.1 0.0 copy-done
  39.1 0.0 copy-done.1
  39.1 15.6 %react.1 = f32[16,152,128]{2,1,0:T(8,128)S(1)} custom-call(f32[16,96,128]{2,1,0:T(8,128)S(1)} %all-to-all-done.recv_ref, f32[16,8,128]{2,1,0:T(8,128)S(1)} %all_to_all.15.lanes_ref, f32[400,128]{1,0:T(8,128)S(1)} %collective-permute-done.message_ref, f32[6,12]{1,0:T(8,128)S(1)} %copy-done, f32[6]{0:T(128)S(1)} %copy-done.1), custom_call_target="tpu_custom_call" | custom-call | tf_op jit(solution)/shard_map/react/pallas_call | solution.py:306
  54.7 23.2 %all_to_all.16.sums_ref = f32[16,152,128]{2,1,0:T(8,128)} all-to-all(f32[16,152,128]{2,1,0:T(8,128)S(1)} %react.1), channel_id=1, replica_groups=mesh['z'=4,'y'=4,'h'=2,'q'=4] {'z','y'}, dimensions={0} | all-to-all | bytes 2490368 | tf_op jit(solution)/shard_map/all_to_all | solution.py:341
  77.8 2.2 %mean.1 = f32[18,4096]{1,0:T(8,128)} custom-call(f32[16,152,128]{2,1,0:T(8,128)} %all_to_all.16.sums_ref), custom_call_target="tpu_custom_call" | custom-call | tf_op jit(solution)/shard_map/mean/pallas_call | solution.py:141
  (1 shorter events, 0.0 us)
Async XLA Ops:
  2.0 37.1 %copy-start = (f32[6,12]{1,0:T(8,128)S(1)}, f32[6,12]{1,0:T(8,128)}, u32[]{:S(2)}) copy-start(f32[6,12]{1,0:T(8,128)} %stoich_ref.1) | copy-start | bytes 868
  2.0 37.1 %copy-start.1 = (f32[6]{0:T(128)S(1)}, f32[6]{0:T(128)}, u32[]{:S(2)}) copy-start(f32[6]{0:T(128)} %logk_ref.1) | copy-start | bytes 76
  2.0 22.8 %all-to-all-start = ((f32[16,96,128]{2,1,0:T(8,128)}), f32[16,96,128]{2,1,0:T(8,128)S(1)}, u32[]{:S(2)}, u32[]{:S(2)}) async-start(f32[16,96,128]{2,1,0:T(8,128)} %cells.1), calls=%async_computation | async-start | bytes 1572864 | tf_op jit(solution)/shard_map/all_to_all | solution.py:335
  12.1 1.6 %collective-permute-start = (f32[400,128]{1,0:T(8,128)}, f32[400,128]{1,0:T(8,128)S(1)}, u32[]{:S(2)}, u32[]{:S(2)}) collective-permute-start(f32[400,128]{1,0:T(8,128)} %pack.1), channel_id=1, source_target_pairs={{0,0},{1,4},{2,32},{3,36},{4,64},{5,68},{6,96},{7,100},{8,8},{9,12... | collective-permute-start | bytes 614408 | tf_op jit(solution)/shard_map/ppermute | solution.py:336

commit v3 on v2

--- a/solution.py
+++ b/solution.py
@@ -77,30 +77,56 @@
     write(cross_ref, [rows[i] * rows[j] for i, j in pairs(NC)], term, same, MOST)
 
 
-def cells_kernel(column_ref, cell_ref, out_ref):
+def cells_kernel(column_ref, cell_ref, pick_ref, out_ref):
     for y in range(SIDE):
         for kt in range(SUB):
             value = cell_ref[:, pl.ds((y * SUB + kt) * WIN, WIN)]
             for z in range(SIDE):
                 out_ref[z * SIDE + y, pl.ds(kt, NC, stride=SUB), :] = value
-
-
-def cells_to_send(column, cell_state):
+    for kt in range(SUB):
+        lanes = jnp.bitwise_and(pick_ref[0, 0, :, pl.ds(kt * WIN, WIN)], WIN - 1).astype(F32)
+        for b in range(FLOW):
+            out_ref[b, pl.ds(NC * SUB + kt, 1), :] = lanes[b : b + 1, :]
+
+
+def cells_to_send(column, cell_state, pick):
     block = SIDE * SUB * WIN
     return pl.pallas_call(
         cells_kernel,
-        out_shape=jax.ShapeDtypeStruct((FLOW, NC * SUB, WIN), F32),
+        out_shape=jax.ShapeDtypeStruct((FLOW, (NC + 1) * SUB, WIN), F32),
         grid_spec=pltpu.PrefetchScalarGridSpec(
             num_scalar_prefetch=1,
             grid=(1,),
-            in_specs=[pl.BlockSpec((NC, block), lambda step, column: (0, column[0]))],
-            out_specs=pl.BlockSpec((FLOW, NC * SUB, WIN), lambda step, column: (0, 0, 0)),
+            in_specs=[
+                pl.BlockSpec((NC, block), lambda step, column: (0, column[0])),
+                pl.BlockSpec((1, 1, FLOW, SUB * WIN), lambda step, column: (0, 0, 0, 0)),
+            ],
+            out_specs=pl.BlockSpec((FLOW, (NC + 1) * SUB, WIN), lambda step, column: (0, 0, 0)),
         ),
         name="cells",
-    )(column, cell_state)
-
-
-def pack_kernel(slot_ref, courant_ref, inflow_ref, pick_ref, message_ref, first_buf, second_buf):
+    )(column, cell_state, pick)
+
+
+def locate_kernel(recv_ref, packed_ref, message_ref):
+    for source in range(FLOW):
+        rows = pl.ds(source * SUB, SUB)
+        lane = recv_ref[source, pl.ds(NC * SUB, SUB), :]
+        message_ref[rows, :] = jnp.take_along_axis(lane, packed_ref[rows, :].astype(jnp.int32), axis=1)
+    rest = pl.ds(WIN, LANES - WIN)
+    message_ref[rest, :] = packed_ref[rest, :]
+
+
+def locate(recv, packed):
+    return pl.pallas_call(
+        locate_kernel,
+        out_shape=jax.ShapeDtypeStruct(packed.shape, F32),
+        in_specs=[pl.BlockSpec(memory_space=pltpu.VMEM)] * 2,
+        compiler_params=pltpu.CompilerParams(vmem_limit_bytes=8 * 1024 * 1024),
+        name="locate",
+    )(recv, packed)
+
+
+def pack_kernel(slot_ref, courant_ref, inflow_ref, message_ref, first_buf, second_buf):
     def rows(ref, buffer, value):
         buffer[...] = jnp.transpose(value)
         even = buffer[pl.ds(0, WIN, stride=2), :]
@@ -113,18 +139,17 @@
     first = inflow_ref[...]
     message_ref[pl.ds(2 * WIN, NC), :] = jnp.concatenate([first, first], axis=1)
     message_ref[pl.ds(2 * WIN + NC, FLOW - NC), :] = jnp.zeros((FLOW - NC, WIN), F32)
-    for kt in range(SUB):
-        part = jnp.bitwise_and(pick_ref[0, 0, :, pl.ds(kt * WIN, WIN)], WIN - 1)
-        message_ref[pl.ds(LANES + kt, FLOW, stride=SUB), :] = part.astype(F32)
-
-
-def pack(node_slot, courant, inflow, pick):
+
+
+def pack(node_slot, courant, inflow):
     return pl.pallas_call(
         pack_kernel,
-        out_shape=jax.ShapeDtypeStruct((LANES + WIN, WIN), F32),
+        out_shape=jax.ShapeDtypeStruct((LANES, WIN), F32),
+        in_specs=[pl.BlockSpec(memory_space=pltpu.VMEM)] * 3,
         scratch_shapes=[pltpu.VMEM((2 * WIN, HALF), F32)] * 2,
+        compiler_params=pltpu.CompilerParams(vmem_limit_bytes=8 * 1024 * 1024),
         name="pack",
-    )(node_slot.T, courant.T, inflow, pick)
+    )(node_slot.T, courant.T, inflow)
 
 
 def mean_kernel(sums_ref, out_ref):
@@ -141,6 +166,8 @@
     return pl.pallas_call(
         mean_kernel,
         out_shape=jax.ShapeDtypeStruct((NQ - 1, SIDE * SUB * WIN), F32),
+        in_specs=[pl.BlockSpec(memory_space=pltpu.VMEM)],
+        compiler_params=pltpu.CompilerParams(vmem_limit_bytes=8 * 1024 * 1024),
         name="mean",
     )(sums)
 
@@ -219,7 +246,7 @@
 
 
 def react_kernel(
-    recv_ref, lanes_ref, message_ref, stoich_ref, logk_ref,
+    recv_ref, message_ref, stoich_ref, logk_ref,
     out_ref, coef, carry, rows_buf, gram_ref, cross_ref, back_ref,
 ):
     build_tables(stoich_ref, gram_ref, cross_ref, back_ref)
@@ -249,8 +276,7 @@
         for b in range(BATCH):
             source = index * BATCH + b
             base = pl.multiple_of(source * SUB, SUB)
-            slot = message_ref[pl.ds(base, SUB), :].astype(jnp.int32)
-            local = jnp.take_along_axis(lanes_ref[source], slot, axis=1).astype(jnp.int32)
+            local = message_ref[pl.ds(base, SUB), :].astype(jnp.int32)
             places.append(local)
             courant = message_ref[pl.ds(base + WIN, SUB), :]
             ratio = 1.0 / (1.0 + courant)
@@ -302,11 +328,11 @@
     lax.fori_loop(0, FLOW // BATCH, step, 0)
 
 
-def react(recv, lanes, message, stoich, logk):
+def react(recv, message, stoich, logk):
     return pl.pallas_call(
         react_kernel,
         out_shape=jax.ShapeDtypeStruct((FLOW, NQ * SUB, WIN), F32),
-        in_specs=[pl.BlockSpec(memory_space=pltpu.VMEM)] * 3
+        in_specs=[pl.BlockSpec(memory_space=pltpu.VMEM)] * 2
         + [pl.BlockSpec(memory_space=pltpu.SMEM)] * 2,
         scratch_shapes=[
             pltpu.VMEM((NX * NC + NX, SUB, WIN), F32),
@@ -316,9 +342,9 @@
             pltpu.VMEM((624, len(MOST) * NX * SUB), BF16),
             pltpu.VMEM((96, len(ALL) * NX * SUB), BF16),
         ],
-        compiler_params=pltpu.CompilerParams(vmem_limit_bytes=48 * 1024 * 1024),
+        compiler_params=pltpu.CompilerParams(vmem_limit_bytes=24 * 1024 * 1024),
         name="react",
-    )(recv, lanes, message, stoich, logk)
+    )(recv, message, stoich, logk)
 
 
 def body(cell_state, inflow, courant, pick, node_slot, stoich, logk):
@@ -331,13 +357,11 @@
                 for h in range(2):
                     source = (z * SIDE + y) * 2 * SIDE + x * 2 + h
                     route.append((source, (x * SIDE + y) * 2 * SIDE + h * SIDE + z))
-    send = cells_to_send(column[None], cell_state)
+    send = cells_to_send(column[None], cell_state, pick)
     recv = lax.all_to_all(send, ("z", "y"), 0, 0, tiled=True)
-    message = lax.ppermute(pack(node_slot, courant, inflow, pick), everywhere, route)
-    lanes = message[LANES:].reshape(FLOW, SUB, WIN)
-    recv, lanes = lax.optimization_barrier((recv, lanes))
-    lanes = lax.all_to_all(lanes, ("q", "y"), 0, 0, tiled=True)
-    sums = react(recv, lanes, message, stoich, logk)
+    packed = pack(node_slot, courant, inflow)
+    message = lax.ppermute(locate(recv, packed), everywhere, route)
+    sums = react(recv, message, stoich, logk)
     back = lax.all_to_all(sums, ("z", "y"), 0, 0, tiled=True)
     return mean(back)
 

time: 80.7 us -> 75.2 us (0.932)
  blocking collectives: 37.4 us -> 32.2 us
  waiting for transfers between devices: 11.1 us -> 15 us
  Pallas kernels: 21.7 us -> 18.7 us
  starting transfers between devices: 9.84 us -> 8.95 us
    all_to_all x1 -> x0, blocking collectives: 14.3 us -> none  [body(): lanes = lax.all_to_all(lanes, ('q', 'y'), 0, 0, tiled=True)]
    all_to_all x1, blocking collectives: 23.2 us -> 32.2 us  [body(): back = lax.all_to_all(sums, ('z', 'y'), 0, 0, tiled=True)]
    all_to_all x1, waiting for transfers between devices: 11.1 us -> 15 us  [body(): recv = lax.all_to_all(send, ('z', 'y'), 0, 0, tiled=True)]
    pallas_call x2 -> x3, Pallas kernels: 3.84 us -> 2.37 us  [the longest x1 2.03 us: cells_to_send(): pl.pallas_call(cells_kernel, out_shape=jax.ShapeDtypeStruct((FLOW, (NC +...]
    pallas_call x1, Pallas kernels: 2.25 us -> 0.96 us  [mean(): pl.pallas_call(mean_kernel, out_shape=jax.ShapeDtypeStruct((NQ - 1, SIDE...]
    ppermute x1, starting transfers between devices: 1.58 us -> 0.67 us  [body(): message = lax.ppermute(locate(recv, packed), everywhere, route)]
  transfers between devices with their start and end apart: 2 -> 2, of which waited for: 1 -> 1; matrix products, arithmetic and copies ran while one was open for 0% -> 0% of each run, Pallas kernels for 2% -> 0%
where the time goes in v3:
time: 75.2 us; the launch traced here: 75 us
  blocking collectives  32.2 us (43%)
  Pallas kernels  18.7 us (25%)
  waiting for transfers between devices  15 us (20%)
  starting transfers between devices  8.95 us (12%)
    all_to_all x1, blocking collectives, body(): back = lax.all_to_all(sums, ('z', 'y'), 0, 0, tiled=True)  32.2 us
    pallas_call x1, Pallas kernels, react(): pl.pallas_call(react_kernel, out_shape=jax.ShapeDtypeStruct((FLOW, NQ * S...  15.3 us
    all_to_all x1, waiting for transfers between devices, body(): recv = lax.all_to_all(send, ('z', 'y'), 0, 0, tiled=True)  15 us
    all_to_all x1, starting transfers between devices, body(): recv = lax.all_to_all(send, ('z', 'y'), 0, 0, tiled=True)  8.28 us
    pallas_call x1, Pallas kernels, cells_to_send(): pl.pallas_call(cells_kernel, out_shape=jax.ShapeDtypeStruct((FLOW, (NC +...  2.03 us
  transfers between devices with their start and end apart: 2, of which 1 were waited for; matrix products, arithmetic and copies ran while one was open for 0% of the time, Pallas kernels for 0%

profile of v3, /device:TPU:0, one launch (start us, length us, event | category | flops | bytes accessed | tf_op | source)
XLA Modules:
  0.0 75.0 jit_solution(965665608408670025)
XLA Ops:
  0.0 2.0 %cells.1 = f32[16,104,128]{2,1,0:T(8,128)} custom-call(s32[1]{0:T(128)} %bitcast.column_ref, f32[12,32768]{1,0:T(8,128)} %cell_ref.1, s32[1,1,16,1024]{3,2,1,0:T(8,128)} %pick_ref.1), custom_call_target="tpu_custom_call" | custom-call | tf_op jit(solution)/shard_map/cells/pallas_call | solution.py:94
  2.0 0.0 copy-start
  2.0 0.0 copy-start.1
  2.0 0.0 copy-start.2
  2.0 0.0 copy-start.3
  2.0 0.0 copy-start.4
  2.1 8.3 %all-to-all-start = ((f32[16,104,128]{2,1,0:T(8,128)}), f32[16,104,128]{2,1,0:T(8,128)S(1)}, u32[]{:S(2)}, u32[]{:S(2)}) async-start(f32[16,104,128]{2,1,0:T(8,128)} %cells.1), calls=%async_computation | async-start | bytes 1703936 | tf_op jit(solution)/shard_map/all_to_all | solution.py:361
  10.3 0.0 copy-done
  10.4 0.0 copy-done.1
  10.4 0.0 copy-done.2
  10.4 0.2 pack.1.packed_ref
  10.6 15.0 %all-to-all-done.recv_ref = f32[16,104,128]{2,1,0:T(8,128)S(1)} async-done(((f32[16,104,128]{2,1,0:T(8,128)}), f32[16,104,128]{2,1,0:T(8,128)S(1)}, u32[]{:S(2)}, u32[]{:S(2)}) %all-to-all-start) | async-done | bytes 852000 | tf_op jit(solution)/shard_map/all_to_all | solution.py:361
  25.6 0.1 locate.1
  25.7 0.7 collective-permute-start
  26.4 0.0 collective-permute-done.message_ref
  26.4 0.0 copy-done.3
  26.4 0.0 copy-done.4
  26.4 15.3 %react.1 = f32[16,152,128]{2,1,0:T(8,128)S(1)} custom-call(f32[16,104,128]{2,1,0:T(8,128)S(1)} %all-to-all-done.recv_ref, f32[272,128]{1,0:T(8,128)S(1)} %collective-permute-done.message_ref, f32[6,12]{1,0:T(8,128)S(1)} %copy-done.3, f32[6]{0:T(128)S(1)} %copy-done.4), custom_call_target="tpu_custom_call" | custom-call | tf_op jit(solution)/shard_map/react/pallas_call | solution.py:332
  41.8 32.2 %all_to_all.10.sums_ref = f32[16,152,128]{2,1,0:T(8,128)S(1)} all-to-all(f32[16,152,128]{2,1,0:T(8,128)S(1)} %react.1), channel_id=1, replica_groups=mesh['z'=4,'y'=4,'h'=2,'q'=4] {'z','y'}, dimensions={0} | all-to-all | bytes 2490368 | tf_op jit(solution)/shard_map/all_to_all | solution.py:365
  74.0 1.0 %mean.1 = f32[18,4096]{1,0:T(8,128)} custom-call(f32[16,152,128]{2,1,0:T(8,128)S(1)} %all_to_all.10.sums_ref), custom_call_target="tpu_custom_call" | custom-call | tf_op jit(solution)/shard_map/mean/pallas_call | solution.py:166
Async XLA Ops:
  2.0 8.3 %copy-start = (s32[256,64]{0,1:T(8,128)S(1)}, s32[256,64]{0,1:T(8,128)}, u32[]{:S(2)}) copy-start(s32[256,64]{0,1:T(8,128)} %param.11) | copy-start | bytes 196612
  2.0 8.3 %copy-start.1 = (f32[256,64]{0,1:T(8,128)S(1)}, f32[256,64]{0,1:T(8,128)}, u32[]{:S(2)}) copy-start(f32[256,64]{0,1:T(8,128)} %param.9) | copy-start | bytes 196612
  2.0 8.3 %copy-start.2 = (f32[12,64]{1,0:T(8,128)S(1)}, f32[12,64]{1,0:T(8,128)}, u32[]{:S(2)}) copy-start(f32[12,64]{1,0:T(8,128)} %inflow_ref.1) | copy-start | bytes 9220
  2.0 24.4 %copy-start.3 = (f32[6,12]{1,0:T(8,128)S(1)}, f32[6,12]{1,0:T(8,128)}, u32[]{:S(2)}) copy-start(f32[6,12]{1,0:T(8,128)} %stoich_ref.1) | copy-start | bytes 868
  2.0 24.4 %copy-start.4 = (f32[6]{0:T(128)S(1)}, f32[6]{0:T(128)}, u32[]{:S(2)}) copy-start(f32[6]{0:T(128)} %logk_ref.1) | copy-start | bytes 76
  2.1 23.6 %all-to-all-start = ((f32[16,104,128]{2,1,0:T(8,128)}), f32[16,104,128]{2,1,0:T(8,128)S(1)}, u32[]{:S(2)}, u32[]{:S(2)}) async-start(f32[16,104,128]{2,1,0:T(8,128)} %cells.1), calls=%async_computation | async-start | bytes 1703936 | tf_op jit(solution)/shard_map/all_to_all | solution.py:361
  25.7 0.7 collective-permute-start

commit v4 on v3

--- a/solution.py
+++ b/solution.py
@@ -107,46 +107,49 @@
     )(column, cell_state, pick)
 
 
-def locate_kernel(recv_ref, packed_ref, message_ref):
+def locate_kernel(recv_ref, slots_ref, lanes_ref):
     for source in range(FLOW):
         rows = pl.ds(source * SUB, SUB)
         lane = recv_ref[source, pl.ds(NC * SUB, SUB), :]
-        message_ref[rows, :] = jnp.take_along_axis(lane, packed_ref[rows, :].astype(jnp.int32), axis=1)
-    rest = pl.ds(WIN, LANES - WIN)
-    message_ref[rest, :] = packed_ref[rest, :]
-
-
-def locate(recv, packed):
+        lanes_ref[rows, :] = jnp.take_along_axis(lane, slots_ref[rows, :], axis=1)
+
+
+def locate(recv, slots):
     return pl.pallas_call(
         locate_kernel,
-        out_shape=jax.ShapeDtypeStruct(packed.shape, F32),
+        out_shape=jax.ShapeDtypeStruct(slots.shape, F32),
         in_specs=[pl.BlockSpec(memory_space=pltpu.VMEM)] * 2,
         compiler_params=pltpu.CompilerParams(vmem_limit_bytes=8 * 1024 * 1024),
         name="locate",
-    )(recv, packed)
-
-
-def pack_kernel(slot_ref, courant_ref, inflow_ref, message_ref, first_buf, second_buf):
+    )(recv, slots)
+
+
+def pack_kernel(slot_ref, courant_ref, inflow_ref, slots_ref, message_ref, first_buf, second_buf):
     def rows(ref, buffer, value):
         buffer[...] = jnp.transpose(value)
         even = buffer[pl.ds(0, WIN, stride=2), :]
         odd = buffer[pl.ds(1, WIN, stride=2), :]
         ref[...] = jnp.concatenate([even, odd], axis=1)
 
-    low = jnp.bitwise_and(slot_ref[...], WIN - 1).astype(F32)
-    rows(message_ref.at[pl.ds(0, WIN)], first_buf, low)
-    rows(message_ref.at[pl.ds(WIN, WIN)], second_buf, courant_ref[...])
+    rows(slots_ref, first_buf, jnp.bitwise_and(slot_ref[...], WIN - 1))
+    rows(message_ref.at[pl.ds(0, WIN)], second_buf, courant_ref[...])
     first = inflow_ref[...]
-    message_ref[pl.ds(2 * WIN, NC), :] = jnp.concatenate([first, first], axis=1)
-    message_ref[pl.ds(2 * WIN + NC, FLOW - NC), :] = jnp.zeros((FLOW - NC, WIN), F32)
+    message_ref[pl.ds(WIN, NC), :] = jnp.concatenate([first, first], axis=1)
+    message_ref[pl.ds(WIN + NC, FLOW - NC), :] = jnp.zeros((FLOW - NC, WIN), F32)
 
 
 def pack(node_slot, courant, inflow):
     return pl.pallas_call(
         pack_kernel,
-        out_shape=jax.ShapeDtypeStruct((LANES, WIN), F32),
+        out_shape=(
+            jax.ShapeDtypeStruct((WIN, WIN), jnp.int32),
+            jax.ShapeDtypeStruct((WIN + FLOW, WIN), F32),
+        ),
         in_specs=[pl.BlockSpec(memory_space=pltpu.VMEM)] * 3,
-        scratch_shapes=[pltpu.VMEM((2 * WIN, HALF), F32)] * 2,
+        scratch_shapes=[
+            pltpu.VMEM((2 * WIN, HALF), jnp.int32),
+            pltpu.VMEM((2 * WIN, HALF), F32),
+        ],
         compiler_params=pltpu.CompilerParams(vmem_limit_bytes=8 * 1024 * 1024),
         name="pack",
     )(node_slot.T, courant.T, inflow)
@@ -231,13 +234,17 @@
     logfree = [jnp.log(t) for t in totals]
     invfree = [1.0 / t for t in totals]
     weights = dot(gram, stack(split(jnp.concatenate(invfree, axis=0), 3), ALL))
-    inverse = [jnp.exp(-jnp.maximum(v, -80.0)) for v in log_complexes(logfree)]
+    logc = log_complexes(logfree)
+    inverse = [jnp.exp(-jnp.maximum(v, -80.0)) for v in logc]
     bound = solve_spd(entries(weights, inverse), [jnp.ones_like(totals[0])] * NX)
     taken = spread(split(jnp.concatenate(bound, axis=0), 3))
     logfree = [x - b * v for x, b, v in zip(logfree, taken, invfree)]
+    logc = [v + (b * e - 1.0) for v, b, e in zip(logc, bound, inverse)]
     for sweep in range(ITERS - 1):
         free = [jnp.exp(x) for x in logfree]
-        complexes = [jnp.exp(v) for v in log_complexes(logfree)]
+        if sweep:
+            logc = log_complexes(logfree)
+        complexes = [jnp.exp(v) for v in logc]
         parts = split(jnp.concatenate(complexes, axis=0), 3)
         jacobian = entries(dot(cross, stack(parts, MOST)), free)
         excess = [(t - f) - b for t, f, b in zip(totals, free, spread(parts))]
@@ -246,7 +253,7 @@
 
 
 def react_kernel(
-    recv_ref, message_ref, stoich_ref, logk_ref,
+    recv_ref, lanes_ref, message_ref, stoich_ref, logk_ref,
     out_ref, coef, carry, rows_buf, gram_ref, cross_ref, back_ref,
 ):
     build_tables(stoich_ref, gram_ref, cross_ref, back_ref)
@@ -254,6 +261,7 @@
     row = lax.broadcasted_iota(jnp.int32, (SUB, WIN), 0)
     cell = lax.broadcasted_iota(jnp.int32, (WIN, WIN), 0)
     odd = lane >= HALF
+    none = jnp.zeros((WIN, WIN), BF16)
     for p in range(NX):
         for i in range(NC):
             coef[p * NC + i] = jnp.full((SUB, WIN), stoich_ref[p, i], F32)
@@ -262,7 +270,7 @@
     for b in range(BATCH):
         rows_buf[pl.ds(b * SUB * PAD + NQ - 1, SUB, stride=PAD), :] = jnp.ones((SUB, WIN), F32)
     for c in range(NC):
-        carry[c] = jnp.broadcast_to(message_ref[pl.ds(2 * WIN + c, 1), :], (SUB, WIN))
+        carry[c] = jnp.broadcast_to(message_ref[pl.ds(WIN + c, 1), :], (SUB, WIN))
 
     def swap(value):
         return pltpu.roll(value, HALF, 1)
@@ -276,9 +284,9 @@
         for b in range(BATCH):
             source = index * BATCH + b
             base = pl.multiple_of(source * SUB, SUB)
-            local = message_ref[pl.ds(base, SUB), :].astype(jnp.int32)
+            local = lanes_ref[pl.ds(base, SUB), :].astype(jnp.int32)
             places.append(local)
-            courant = message_ref[pl.ds(base + WIN, SUB), :]
+            courant = message_ref[pl.ds(base, SUB), :]
             ratio = 1.0 / (1.0 + courant)
             weight = courant * ratio
             pair = jnp.where(odd, weight * swap(weight), weight)
@@ -312,27 +320,35 @@
                     :, b * WIN : (b + 1) * WIN
                 ]
         for b in range(BATCH):
-            for kt in range(SUB):
-                hot = (cell == jnp.broadcast_to(places[b][kt : kt + 1, :], (WIN, WIN))).astype(BF16)
-                value = rows_buf[pl.ds((b * SUB + kt) * PAD, PAD), :]
+            for kt in range(0, SUB, 2):
+                hots, values = [], []
+                for k in (kt, kt + 1):
+                    place = jnp.broadcast_to(places[b][k : k + 1, :], (WIN, WIN))
+                    hots.append((cell == place).astype(BF16))
+                    value = rows_buf[pl.ds((b * SUB + k) * PAD, PAD), :]
+                    values.append(jnp.concatenate(split(value, 2), axis=0))
+                upper = jnp.concatenate([hots[0], none], axis=1)
+                hot = jnp.concatenate([upper, jnp.concatenate([none, hots[1]], axis=1)], axis=0)
                 both = lax.dot_general(
-                    jnp.concatenate(split(value, 2), axis=0),
+                    jnp.concatenate(values, axis=1),
                     hot,
                     (((1,), (1,)), ((), ())),
                     preferred_element_type=F32,
                 )
                 sums = both[:PAD] + both[PAD:]
-                out_ref[index * BATCH + b, pl.ds(kt, NQ, stride=SUB), :] = sums[:NQ]
+                for k in (0, 1):
+                    part = sums[:NQ, k * WIN : (k + 1) * WIN]
+                    out_ref[index * BATCH + b, pl.ds(kt + k, NQ, stride=SUB), :] = part
         return unused
 
     lax.fori_loop(0, FLOW // BATCH, step, 0)
 
 
-def react(recv, message, stoich, logk):
+def react(recv, lanes, message, stoich, logk):
     return pl.pallas_call(
         react_kernel,
         out_shape=jax.ShapeDtypeStruct((FLOW, NQ * SUB, WIN), F32),
-        in_specs=[pl.BlockSpec(memory_space=pltpu.VMEM)] * 2
+        in_specs=[pl.BlockSpec(memory_space=pltpu.VMEM)] * 3
         + [pl.BlockSpec(memory_space=pltpu.SMEM)] * 2,
         scratch_shapes=[
             pltpu.VMEM((NX * NC + NX, SUB, WIN), F32),
@@ -344,7 +360,7 @@
         ],
         compiler_params=pltpu.CompilerParams(vmem_limit_bytes=24 * 1024 * 1024),
         name="react",
-    )(recv, message, stoich, logk)
+    )(recv, lanes, message, stoich, logk)
 
 
 def body(cell_state, inflow, courant, pick, node_slot, stoich, logk):
@@ -359,9 +375,10 @@
                     route.append((source, (x * SIDE + y) * 2 * SIDE + h * SIDE + z))
     send = cells_to_send(column[None], cell_state, pick)
     recv = lax.all_to_all(send, ("z", "y"), 0, 0, tiled=True)
-    packed = pack(node_slot, courant, inflow)
-    message = lax.ppermute(locate(recv, packed), everywhere, route)
-    sums = react(recv, message, stoich, logk)
+    slots, message = pack(node_slot, courant, inflow)
+    message = lax.ppermute(message, everywhere, route)
+    lanes = lax.ppermute(locate(recv, slots), everywhere, route)
+    sums = react(recv, lanes, message, stoich, logk)
     back = lax.all_to_all(sums, ("z", "y"), 0, 0, tiled=True)
     return mean(back)
 

time: 75.2 us -> 73.3 us (0.975)
  Pallas kernels: 18.7 us -> 17.4 us
    pallas_call x1, Pallas kernels: 15.3 us -> 14.1 us  [react(): pl.pallas_call(react_kernel, out_shape=jax.ShapeDtypeStruct((FLOW, NQ * S...]
  transfers between devices with their start and end apart: 2 -> 3, of which waited for: 1 -> 1; matrix products, arithmetic and copies ran while one was open for 0% -> 0% of each run, Pallas kernels for 0% -> 0%
where the time goes in v4:
time: 73.3 us; the launch traced here: 73 us
  blocking collectives  31.5 us (43%)
  Pallas kernels  17.4 us (24%)
  waiting for transfers between devices  14.3 us (20%)
  starting transfers between devices  9.62 us (13%)
    all_to_all x1, blocking collectives, body(): back = lax.all_to_all(sums, ('z', 'y'), 0, 0, tiled=True)  31.5 us
    all_to_all x1, waiting for transfers between devices, body(): recv = lax.all_to_all(send, ('z', 'y'), 0, 0, tiled=True)  14.3 us
    pallas_call x1, Pallas kernels, react(): pl.pallas_call(react_kernel, out_shape=jax.ShapeDtypeStruct((FLOW, NQ * S...  14.1 us
    all_to_all x1, starting transfers between devices, body(): recv = lax.all_to_all(send, ('z', 'y'), 0, 0, tiled=True)  8.28 us
    pallas_call x1, Pallas kernels, cells_to_send(): pl.pallas_call(cells_kernel, out_shape=jax.ShapeDtypeStruct((FLOW, (NC +...  2.04 us
  transfers between devices with their start and end apart: 3, of which 1 were waited for; matrix products, arithmetic and copies ran while one was open for 0% of the time, Pallas kernels for 0%

profile of v4, /device:TPU:0, one launch (start us, length us, event | category | flops | bytes accessed | tf_op | source)
XLA Modules:
  0.0 73.0 jit_solution(371031897810291272)
XLA Ops:
  0.0 2.0 %cells.1 = f32[16,104,128]{2,1,0:T(8,128)} custom-call(s32[1]{0:T(128)} %bitcast.column_ref, f32[12,32768]{1,0:T(8,128)} %cell_ref.1, s32[1,1,16,1024]{3,2,1,0:T(8,128)} %pick_ref.1), custom_call_target="tpu_custom_call" | custom-call | tf_op jit(solution)/shard_map/cells/pallas_call | solution.py:94
  2.0 0.0 copy-start
  2.0 0.0 copy-start.1
  2.0 0.0 copy-start.2
  2.0 0.0 copy-start.3
  2.1 0.0 copy-start.4
  2.1 8.3 %all-to-all-start = ((f32[16,104,128]{2,1,0:T(8,128)}), f32[16,104,128]{2,1,0:T(8,128)S(1)}, u32[]{:S(2)}, u32[]{:S(2)}) async-start(f32[16,104,128]{2,1,0:T(8,128)} %cells.1), calls=%async_computation | async-start | bytes 1703936 | tf_op jit(solution)/shard_map/all_to_all | solution.py:377
  10.3 0.0 copy-done
  10.4 0.0 copy-done.1
  10.4 0.0 copy-done.2
  10.4 0.2 pack.1
  10.6 0.7 collective-permute-start.1
  11.3 14.3 %all-to-all-done.recv_ref = f32[16,104,128]{2,1,0:T(8,128)S(1)} async-done(((f32[16,104,128]{2,1,0:T(8,128)}), f32[16,104,128]{2,1,0:T(8,128)S(1)}, u32[]{:S(2)}, u32[]{:S(2)}) %all-to-all-start) | async-done | bytes 852000 | tf_op jit(solution)/shard_map/all_to_all | solution.py:377
  25.6 0.1 locate.1
  25.7 0.7 collective-permute-start
  26.4 0.0 collective-permute-done.1.message_ref
  26.4 0.0 collective-permute-done.lanes_ref
  26.4 0.0 copy-done.3
  26.4 0.0 copy-done.4
  26.4 14.1 %react.1 = f32[16,152,128]{2,1,0:T(8,128)S(1)} custom-call(f32[16,104,128]{2,1,0:T(8,128)S(1)} %all-to-all-done.recv_ref, f32[128,128]{1,0:T(8,128)S(1)} %collective-permute-done.lanes_ref, f32[144,128]{1,0:T(8,128)S(1)} %collective-permute-done.1.message_ref, f32[6,12]{1,0:T(8,128)S(1)} %copy-done.3, f32[6]{0:T(128)S(1)} %copy-done.4), custom_call_target="tpu_custom_call" | custom-call | tf_op jit(solution)/shard_map/react/pallas_call | solution.py:348
  40.5 31.5 %all_to_all.10.sums_ref = f32[16,152,128]{2,1,0:T(8,128)S(1)} all-to-all(f32[16,152,128]{2,1,0:T(8,128)S(1)} %react.1), channel_id=1, replica_groups=mesh['z'=4,'y'=4,'h'=2,'q'=4] {'z','y'}, dimensions={0} | all-to-all | bytes 2490368 | tf_op jit(solution)/shard_map/all_to_all | solution.py:382
  72.0 1.0 %mean.1 = f32[18,4096]{1,0:T(8,128)} custom-call(f32[16,152,128]{2,1,0:T(8,128)S(1)} %all_to_all.10.sums_ref), custom_call_target="tpu_custom_call" | custom-call | tf_op jit(solution)/shard_map/mean/pallas_call | solution.py:169
Async XLA Ops:
  2.0 8.3 %copy-start = (s32[256,64]{0,1:T(8,128)S(1)}, s32[256,64]{0,1:T(8,128)}, u32[]{:S(2)}) copy-start(s32[256,64]{0,1:T(8,128)} %param.11) | copy-start | bytes 196612
  2.0 8.3 %copy-start.1 = (f32[256,64]{0,1:T(8,128)S(1)}, f32[256,64]{0,1:T(8,128)}, u32[]{:S(2)}) copy-start(f32[256,64]{0,1:T(8,128)} %param.9) | copy-start | bytes 196612
  2.0 8.3 %copy-start.2 = (f32[12,64]{1,0:T(8,128)S(1)}, f32[12,64]{1,0:T(8,128)}, u32[]{:S(2)}) copy-start(f32[12,64]{1,0:T(8,128)} %inflow_ref.1) | copy-start | bytes 9220
  2.0 24.4 %copy-start.3 = (f32[6,12]{1,0:T(8,128)S(1)}, f32[6,12]{1,0:T(8,128)}, u32[]{:S(2)}) copy-start(f32[6,12]{1,0:T(8,128)} %stoich_ref.1) | copy-start | bytes 868
  2.1 24.4 %copy-start.4 = (f32[6]{0:T(128)S(1)}, f32[6]{0:T(128)}, u32[]{:S(2)}) copy-start(f32[6]{0:T(128)} %logk_ref.1) | copy-start | bytes 76
  2.1 23.6 %all-to-all-start = ((f32[16,104,128]{2,1,0:T(8,128)}), f32[16,104,128]{2,1,0:T(8,128)S(1)}, u32[]{:S(2)}, u32[]{:S(2)}) async-start(f32[16,104,128]{2,1,0:T(8,128)} %cells.1), calls=%async_computation | async-start | bytes 1703936 | tf_op jit(solution)/shard_map/all_to_all | solution.py:377
  10.6 15.8 %collective-permute-start.1 = (f32[144,128]{1,0:T(8,128)S(1)}, f32[144,128]{1,0:T(8,128)S(1)}, u32[]{:S(2)}, u32[]{:S(2)}) collective-permute-start(f32[144,128]{1,0:T(8,128)S(1)} %get-tuple-element.8), channel_id=1, source_target_pairs={{0,0},{1,4},{2,32},{3,36},{4,64},{5,68},{6,96},{7,100},{8,8},{9,12... | collective-permute-start | bytes 221192 | tf_op jit(solution)/shard_map/ppermute | solution.py:379
  25.7 0.7 collective-permute-start

commit v5 on v4

--- a/solution.py
+++ b/solution.py
@@ -77,7 +77,21 @@
     write(cross_ref, [rows[i] * rows[j] for i, j in pairs(NC)], term, same, MOST)
 
 
-def cells_kernel(column_ref, cell_ref, pick_ref, out_ref):
+def tables(stoich):
+    return pl.pallas_call(
+        build_tables,
+        out_shape=(
+            jax.ShapeDtypeStruct((176, len(ALL) * NC * SUB), BF16),
+            jax.ShapeDtypeStruct((624, len(MOST) * NX * SUB), BF16),
+            jax.ShapeDtypeStruct((96, len(ALL) * NX * SUB), BF16),
+        ),
+        in_specs=[pl.BlockSpec(memory_space=pltpu.SMEM)],
+        compiler_params=pltpu.CompilerParams(vmem_limit_bytes=8 * 1024 * 1024),
+        name="tables",
+    )(stoich)
+
+
+def cells_kernel(column_ref, cell_ref, pick_ref, out_ref, lanes_ref):
     for y in range(SIDE):
         for kt in range(SUB):
             value = cell_ref[:, pl.ds((y * SUB + kt) * WIN, WIN)]
@@ -85,8 +99,9 @@
                 out_ref[z * SIDE + y, pl.ds(kt, NC, stride=SUB), :] = value
     for kt in range(SUB):
         lanes = jnp.bitwise_and(pick_ref[0, 0, :, pl.ds(kt * WIN, WIN)], WIN - 1).astype(F32)
-        for b in range(FLOW):
-            out_ref[b, pl.ds(NC * SUB + kt, 1), :] = lanes[b : b + 1, :]
+        lanes_ref[pl.ds(kt, FLOW, stride=SUB), :] = lanes
+    for b in range(FLOW):
+        out_ref[b, pl.ds(NC * SUB, SUB), :] = lanes_ref[pl.ds(b * SUB, SUB), :]
 
 
 def cells_to_send(column, cell_state, pick):
@@ -102,6 +117,7 @@
                 pl.BlockSpec((1, 1, FLOW, SUB * WIN), lambda step, column: (0, 0, 0, 0)),
             ],
             out_specs=pl.BlockSpec((FLOW, (NC + 1) * SUB, WIN), lambda step, column: (0, 0, 0)),
+            scratch_shapes=[pltpu.VMEM((FLOW * SUB, WIN), F32)],
         ),
         name="cells",
     )(column, cell_state, pick)
@@ -253,10 +269,9 @@
 
 
 def react_kernel(
-    recv_ref, lanes_ref, message_ref, stoich_ref, logk_ref,
-    out_ref, coef, carry, rows_buf, gram_ref, cross_ref, back_ref,
+    recv_ref, lanes_ref, message_ref, gram_ref, cross_ref, back_ref, stoich_ref, logk_ref,
+    out_ref, coef, carry, rows_buf,
 ):
-    build_tables(stoich_ref, gram_ref, cross_ref, back_ref)
     lane = lax.broadcasted_iota(jnp.int32, (SUB, WIN), 1)
     row = lax.broadcasted_iota(jnp.int32, (SUB, WIN), 0)
     cell = lax.broadcasted_iota(jnp.int32, (WIN, WIN), 0)
@@ -344,23 +359,20 @@
     lax.fori_loop(0, FLOW // BATCH, step, 0)
 
 
-def react(recv, lanes, message, stoich, logk):
+def react(recv, lanes, message, coefficients, stoich, logk):
     return pl.pallas_call(
         react_kernel,
         out_shape=jax.ShapeDtypeStruct((FLOW, NQ * SUB, WIN), F32),
-        in_specs=[pl.BlockSpec(memory_space=pltpu.VMEM)] * 3
+        in_specs=[pl.BlockSpec(memory_space=pltpu.VMEM)] * 6
         + [pl.BlockSpec(memory_space=pltpu.SMEM)] * 2,
         scratch_shapes=[
             pltpu.VMEM((NX * NC + NX, SUB, WIN), F32),
             pltpu.VMEM((NC, SUB, WIN), F32),
             pltpu.VMEM((BATCH * SUB * PAD, WIN), F32),
-            pltpu.VMEM((176, len(ALL) * NC * SUB), BF16),
-            pltpu.VMEM((624, len(MOST) * NX * SUB), BF16),
-            pltpu.VMEM((96, len(ALL) * NX * SUB), BF16),
         ],
         compiler_params=pltpu.CompilerParams(vmem_limit_bytes=24 * 1024 * 1024),
         name="react",
-    )(recv, lanes, message, stoich, logk)
+    )(recv, lanes, message, *coefficients, stoich, logk)
 
 
 def body(cell_state, inflow, courant, pick, node_slot, stoich, logk):
@@ -372,13 +384,15 @@
             for x in range(SIDE):
                 for h in range(2):
                     source = (z * SIDE + y) * 2 * SIDE + x * 2 + h
-                    route.append((source, (x * SIDE + y) * 2 * SIDE + h * SIDE + z))
+                    away = (x - 2 * h - z // 2) % SIDE
+                    to = (z + (2, 1, 0, 3)[away]) % SIDE
+                    route.append((source, (to * SIDE + y) * 2 * SIDE + h * SIDE + z))
     send = cells_to_send(column[None], cell_state, pick)
     recv = lax.all_to_all(send, ("z", "y"), 0, 0, tiled=True)
     slots, message = pack(node_slot, courant, inflow)
     message = lax.ppermute(message, everywhere, route)
     lanes = lax.ppermute(locate(recv, slots), everywhere, route)
-    sums = react(recv, lanes, message, stoich, logk)
+    sums = react(recv, lanes, message, tables(stoich), stoich, logk)
     back = lax.all_to_all(sums, ("z", "y"), 0, 0, tiled=True)
     return mean(back)
 

time: 73.3 us -> 69.3 us (0.945); the launches traced: 73 us -> 68.2 us
  blocking collectives: 31.5 us -> 21.9 us
  starting transfers between devices: 9.62 us -> 13.3 us
  Pallas kernels: 17.4 us -> 18.2 us
    all_to_all x1, blocking collectives: 31.5 us -> 21.9 us  [body(): back = lax.all_to_all(sums, ('z', 'y'), 0, 0, tiled=True)]
    ppermute x1, waiting for transfers between devices: 0.01 us -> 3.16 us  [body(): lanes = lax.ppermute(locate(recv, slots), everywhere, route)]
    ppermute x1, starting transfers between devices: 0.67 us -> 3.5 us  [body(): message = lax.ppermute(message, everywhere, route)]
    all_to_all x1, waiting for transfers between devices: 14.3 us -> 11.5 us  [body(): recv = lax.all_to_all(send, ('z', 'y'), 0, 0, tiled=True)]
    pallas_call x0 -> x1, Pallas kernels: none -> 1.22 us  [tables(): pl.pallas_call(build_tables, out_shape=(jax.ShapeDtypeStruct((176, len(AL...]
    ppermute x1, starting transfers between devices: 0.68 us -> 1.55 us  [body(): lanes = lax.ppermute(locate(recv, slots), everywhere, route)]
  transfers between devices with their start and end apart: 3 -> 3, of which waited for: 1 -> 2; matrix products, arithmetic and copies ran while one was open for 0% -> 0% of each run, Pallas kernels for 0% -> 2%
where the time goes in v5:
time: 69.3 us; the launch traced here: 68.2 us
  blocking collectives  21.9 us (32%)
  Pallas kernels  18.2 us (26%)
  waiting for transfers between devices  14.7 us (21%)
  starting transfers between devices  13.3 us (19%)
    all_to_all x1, blocking collectives, body(): back = lax.all_to_all(sums, ('z', 'y'), 0, 0, tiled=True)  21.9 us
    pallas_call x1, Pallas kernels, react(): pl.pallas_call(react_kernel, out_shape=jax.ShapeDtypeStruct((FLOW, NQ * S...  13.7 us
    all_to_all x1, waiting for transfers between devices, body(): recv = lax.all_to_all(send, ('z', 'y'), 0, 0, tiled=True)  11.5 us
    all_to_all x1, starting transfers between devices, body(): recv = lax.all_to_all(send, ('z', 'y'), 0, 0, tiled=True)  8.28 us
    ppermute x1, starting transfers between devices, body(): message = lax.ppermute(message, everywhere, route)  3.5 us
    ppermute x1, waiting for transfers between devices, body(): lanes = lax.ppermute(locate(recv, slots), everywhere, route)  3.16 us
    pallas_call x1, Pallas kernels, cells_to_send(): pl.pallas_call(cells_kernel, out_shape=jax.ShapeDtypeStruct((FLOW, (NC +...  2.06 us
    ppermute x1, starting transfers between devices, body(): lanes = lax.ppermute(locate(recv, slots), everywhere, route)  1.55 us
  transfers between devices with their start and end apart: 3, of which 2 were waited for; matrix products, arithmetic and copies ran while one was open for 0% of the time, Pallas kernels for 2%

profile of v5, /device:TPU:0, one launch (start us, length us, event | category | flops | bytes accessed | tf_op | source)
XLA Modules:
  0.0 68.2 jit_solution(7375291606642289927)
XLA Ops:
  0.0 2.1 %cells.1 = f32[16,104,128]{2,1,0:T(8,128)} custom-call(s32[1]{0:T(128)} %bitcast.column_ref, f32[12,32768]{1,0:T(8,128)} %cell_ref.1, s32[1,1,16,1024]{3,2,1,0:T(8,128)} %pick_ref.1), custom_call_target="tpu_custom_call" | custom-call | tf_op jit(solution)/shard_map/cells/pallas_call | solution.py:109
  2.1 0.0 copy-start
  2.1 0.0 copy-start.1
  2.1 0.0 copy-start.3
  2.1 0.0 copy-start.2
  2.1 0.0 copy-start.4
  2.1 8.3 %all-to-all-start = ((f32[16,104,128]{2,1,0:T(8,128)}), f32[16,104,128]{2,1,0:T(8,128)S(1)}, u32[]{:S(2)}, u32[]{:S(2)}) async-start(f32[16,104,128]{2,1,0:T(8,128)} %cells.1), calls=%async_computation | async-start | bytes 1703936 | tf_op jit(solution)/shard_map/all_to_all | solution.py:391
  10.4 0.0 copy-done
  10.4 0.0 copy-done.1
  10.4 0.0 copy-done.3
  10.4 0.2 pack.1
  10.6 3.5 %collective-permute-start.1 = (f32[144,128]{1,0:T(8,128)S(1)}, f32[144,128]{1,0:T(8,128)S(1)}, u32[]{:S(2)}, u32[]{:S(2)}) collective-permute-start(f32[144,128]{1,0:T(8,128)S(1)} %get-tuple-element.11), channel_id=1, source_target_pairs={{0,64},{1,4},{2,32},{3,100},{4,0},{5,68},{6,96},{7,36},{8,72},{9,1... | collective-permute-start | bytes 221192 | tf_op jit(solution)/shard_map/ppermute | solution.py:393
  14.2 11.5 %all-to-all-done.recv_ref = f32[16,104,128]{2,1,0:T(8,128)S(1)} async-done(((f32[16,104,128]{2,1,0:T(8,128)}), f32[16,104,128]{2,1,0:T(8,128)S(1)}, u32[]{:S(2)}, u32[]{:S(2)}) %all-to-all-start) | async-done | bytes 852000 | tf_op jit(solution)/shard_map/all_to_all | solution.py:391
  25.6 0.1 locate.1
  25.7 1.6 %collective-permute-start = (f32[128,128]{1,0:T(8,128)S(1)}, f32[128,128]{1,0:T(8,128)S(1)}, u32[]{:S(2)}, u32[]{:S(2)}) collective-permute-start(f32[128,128]{1,0:T(8,128)S(1)} %locate.1), channel_id=1, source_target_pairs={{0,64},{1,4},{2,32},{3,100},{4,0},{5,68},{6,96},{7,36},{8,72},{9,1... | collective-permute-start | bytes 196616 | tf_op jit(solution)/shard_map/ppermute | solution.py:394
  27.3 0.0 copy-done.2
  27.3 1.2 %tables.1 = (bf16[176,576]{1,0:T(8,128)(2,1)S(1)}, bf16[624,240]{1,0:T(8,128)(2,1)S(1)}, bf16[96,288]{1,0:T(8,128)(2,1)S(1)}) custom-call(f32[6,12]{1,0:T(8,128)S(1)} %copy-done.2), custom_call_target="tpu_custom_call" | custom-call | tf_op jit(solution)/shard_map/tables/pallas_call | solution.py:81
  28.5 0.0 collective-permute-done.1.message_ref
  28.5 3.2 %collective-permute-done.lanes_ref = f32[128,128]{1,0:T(8,128)S(1)} collective-permute-done((f32[128,128]{1,0:T(8,128)S(1)}, f32[128,128]{1,0:T(8,128)S(1)}, u32[]{:S(2)}, u32[]{:S(2)}) %collective-permute-start) | collective-permute-done | bytes 65568 | tf_op jit(solution)/shard_map/ppermute | solution.py:394
  31.7 0.0 copy-done.4
  31.7 13.7 %react.1 = f32[16,152,128]{2,1,0:T(8,128)S(1)} custom-call(f32[16,104,128]{2,1,0:T(8,128)S(1)} %all-to-all-done.recv_ref, f32[128,128]{1,0:T(8,128)S(1)} %collective-permute-done.lanes_ref, f32[144,128]{1,0:T(8,128)S(1)} %collective-permute-done.1.message_ref, bf16[176,576]{1,0:T(8,128)(2,1)S(1)} %get-tuple-element.12.gram_ref, ...), custom_call_target="tpu_custom_call" | custom-call | tf_op jit(solution)/shard_map/react/pallas_call | solution.py:363
  45.3 21.9 %all_to_all.10.sums_ref = f32[16,152,128]{2,1,0:T(8,128)S(1)} all-to-all(f32[16,152,128]{2,1,0:T(8,128)S(1)} %react.1), channel_id=1, replica_groups=mesh['z'=4,'y'=4,'h'=2,'q'=4] {'z','y'}, dimensions={0} | all-to-all | bytes 2490368 | tf_op jit(solution)/shard_map/all_to_all | solution.py:396
  67.3 1.0 %mean.1 = f32[18,4096]{1,0:T(8,128)} custom-call(f32[16,152,128]{2,1,0:T(8,128)S(1)} %all_to_all.10.sums_ref), custom_call_target="tpu_custom_call" | custom-call | tf_op jit(solution)/shard_map/mean/pallas_call | solution.py:185
Async XLA Ops:
  2.1 8.3 %copy-start = (s32[256,64]{0,1:T(8,128)S(1)}, s32[256,64]{0,1:T(8,128)}, u32[]{:S(2)}) copy-start(s32[256,64]{0,1:T(8,128)} %param.11) | copy-start | bytes 196612
  2.1 8.3 %copy-start.1 = (f32[256,64]{0,1:T(8,128)S(1)}, f32[256,64]{0,1:T(8,128)}, u32[]{:S(2)}) copy-start(f32[256,64]{0,1:T(8,128)} %param.9) | copy-start | bytes 196612
  2.1 8.3 %copy-start.3 = (f32[12,64]{1,0:T(8,128)S(1)}, f32[12,64]{1,0:T(8,128)}, u32[]{:S(2)}) copy-start(f32[12,64]{1,0:T(8,128)} %inflow_ref.1) | copy-start | bytes 9220
  2.1 25.2 %copy-start.2 = (f32[6,12]{1,0:T(8,128)S(1)}, f32[6,12]{1,0:T(8,128)}, u32[]{:S(2)}) copy-start(f32[6,12]{1,0:T(8,128)} %stoich_ref.3) | copy-start | bytes 868
  2.1 29.6 %copy-start.4 = (f32[6]{0:T(128)S(1)}, f32[6]{0:T(128)}, u32[]{:S(2)}) copy-start(f32[6]{0:T(128)} %logk_ref.1) | copy-start | bytes 76
  2.1 23.6 %all-to-all-start = ((f32[16,104,128]{2,1,0:T(8,128)}), f32[16,104,128]{2,1,0:T(8,128)S(1)}, u32[]{:S(2)}, u32[]{:S(2)}) async-start(f32[16,104,128]{2,1,0:T(8,128)} %cells.1), calls=%async_computation | async-start | bytes 1703936 | tf_op jit(solution)/shard_map/all_to_all | solution.py:391
  10.6 17.9 %collective-permute-start.1 = (f32[144,128]{1,0:T(8,128)S(1)}, f32[144,128]{1,0:T(8,128)S(1)}, u32[]{:S(2)}, u32[]{:S(2)}) collective-permute-start(f32[144,128]{1,0:T(8,128)S(1)} %get-tuple-element.11), channel_id=1, source_target_pairs={{0,64},{1,4},{2,32},{3,100},{4,0},{5,68},{6,96},{7,36},{8,72},{9,1... | collective-permute-start | bytes 221192 | tf_op jit(solution)/shard_map/ppermute | solution.py:393
  25.7 5.9 %collective-permute-start = (f32[128,128]{1,0:T(8,128)S(1)}, f32[128,128]{1,0:T(8,128)S(1)}, u32[]{:S(2)}, u32[]{:S(2)}) collective-permute-start(f32[128,128]{1,0:T(8,128)S(1)} %locate.1), channel_id=1, source_target_pairs={{0,64},{1,4},{2,32},{3,100},{4,0},{5,68},{6,96},{7,36},{8,72},{9,1... | collective-permute-start | bytes 196616 | tf_op jit(solution)/shard_map/ppermute | solution.py:394

commit v6 on v5

--- a/solution.py
+++ b/solution.py
@@ -91,12 +91,16 @@
     )(stoich)
 
 
-def cells_kernel(column_ref, cell_ref, pick_ref, out_ref, lanes_ref):
+def cells_kernel(column_ref, cell_ref, pick_ref, out_ref, lanes_ref, part_ref):
+    blank = jnp.zeros((FLOW - NC, WIN), F32)
     for y in range(SIDE):
         for kt in range(SUB):
             value = cell_ref[:, pl.ds((y * SUB + kt) * WIN, WIN)]
-            for z in range(SIDE):
-                out_ref[z * SIDE + y, pl.ds(kt, NC, stride=SUB), :] = value
+            value = jnp.concatenate([value, blank], axis=0)
+            part_ref[y, pl.ds(kt, FLOW, stride=SUB), :] = value
+        for z in range(SIDE):
+            rows = pl.ds(0, NC * SUB)
+            out_ref[z * SIDE + y, rows, :] = part_ref[y, rows, :]
     for kt in range(SUB):
         lanes = jnp.bitwise_and(pick_ref[0, 0, :, pl.ds(kt * WIN, WIN)], WIN - 1).astype(F32)
         lanes_ref[pl.ds(kt, FLOW, stride=SUB), :] = lanes
@@ -117,7 +121,10 @@
                 pl.BlockSpec((1, 1, FLOW, SUB * WIN), lambda step, column: (0, 0, 0, 0)),
             ],
             out_specs=pl.BlockSpec((FLOW, (NC + 1) * SUB, WIN), lambda step, column: (0, 0, 0)),
-            scratch_shapes=[pltpu.VMEM((FLOW * SUB, WIN), F32)],
+            scratch_shapes=[
+                pltpu.VMEM((FLOW * SUB, WIN), F32),
+                pltpu.VMEM((SIDE, FLOW * SUB, WIN), F32),
+            ],
         ),
         name="cells",
     )(column, cell_state, pick)
@@ -171,14 +178,21 @@
     )(node_slot.T, courant.T, inflow)
 
 
-def mean_kernel(sums_ref, out_ref):
+def mean_kernel(sums_ref, out_ref, rows_buf):
     for y in range(SIDE):
+        totals = []
+        for q in range(NQ):
+            rows = pl.ds(q * SUB, SUB)
+            total = sums_ref[y, rows, :]
+            for z in range(1, SIDE):
+                total = total + sums_ref[z * SIDE + y, rows, :]
+            totals.append(total)
+        share = 1.0 / jnp.maximum(totals[NQ - 1], 1.0)
+        for q in range(NQ - 1):
+            rows_buf[y, pl.ds(q, SUB, stride=PAD), :] = totals[q] * share
         for kt in range(SUB):
-            total = sums_ref[y, pl.ds(kt, NQ, stride=SUB), :]
-            for z in range(1, SIDE):
-                total = total + sums_ref[z * SIDE + y, pl.ds(kt, NQ, stride=SUB), :]
-            share = 1.0 / jnp.maximum(total[NQ - 1 :, :], 1.0)
-            out_ref[:, pl.ds((y * SUB + kt) * WIN, WIN)] = total[: NQ - 1] * share
+            part = rows_buf[y, pl.ds(kt * PAD, PAD), :]
+            out_ref[:, pl.ds((y * SUB + kt) * WIN, WIN)] = part[: NQ - 1]
 
 
 def mean(sums):
@@ -186,6 +200,7 @@
         mean_kernel,
         out_shape=jax.ShapeDtypeStruct((NQ - 1, SIDE * SUB * WIN), F32),
         in_specs=[pl.BlockSpec(memory_space=pltpu.VMEM)],
+        scratch_shapes=[pltpu.VMEM((SIDE, SUB * PAD, WIN), F32)],
         compiler_params=pltpu.CompilerParams(vmem_limit_bytes=8 * 1024 * 1024),
         name="mean",
     )(sums)
@@ -270,7 +285,7 @@
 
 def react_kernel(
     recv_ref, lanes_ref, message_ref, gram_ref, cross_ref, back_ref, stoich_ref, logk_ref,
-    out_ref, coef, carry, rows_buf,
+    out_ref, coef, carry, rows_buf, sums_buf,
 ):
     lane = lax.broadcasted_iota(jnp.int32, (SUB, WIN), 1)
     row = lax.broadcasted_iota(jnp.int32, (SUB, WIN), 0)
@@ -325,7 +340,7 @@
             [jnp.concatenate(parts, axis=1) for parts in moved],
             lambda p, i: wide(coef[p * NC + i]),
             lambda p: wide(coef[NX * NC + p]),
-            gram_ref[:168],
+            gram_ref[...],
             cross_ref[...],
             back_ref[...],
         )
@@ -352,8 +367,9 @@
                 )
                 sums = both[:PAD] + both[PAD:]
                 for k in (0, 1):
-                    part = sums[:NQ, k * WIN : (k + 1) * WIN]
-                    out_ref[index * BATCH + b, pl.ds(kt + k, NQ, stride=SUB), :] = part
+                    part = sums[:, k * WIN : (k + 1) * WIN]
+                    sums_buf[b, pl.ds(kt + k, PAD, stride=SUB), :] = part
+            out_ref[index * BATCH + b] = sums_buf[b, pl.ds(0, NQ * SUB), :]
         return unused
 
     lax.fori_loop(0, FLOW // BATCH, step, 0)
@@ -369,6 +385,7 @@
             pltpu.VMEM((NX * NC + NX, SUB, WIN), F32),
             pltpu.VMEM((NC, SUB, WIN), F32),
             pltpu.VMEM((BATCH * SUB * PAD, WIN), F32),
+            pltpu.VMEM((BATCH, SUB * PAD, WIN), F32),
         ],
         compiler_params=pltpu.CompilerParams(vmem_limit_bytes=24 * 1024 * 1024),
         name="react",

time: 69.3 us -> 69.2 us (level)
  no operation moved by 1% of the time
where the time goes in v6:
time: 69.2 us; the launch traced here: 68.2 us
  blocking collectives  21.9 us (32%)
  Pallas kernels  18.1 us (26%)
  waiting for transfers between devices  14.7 us (21%)
  starting transfers between devices  13.3 us (19%)
    all_to_all x1, blocking collectives, body(): back = lax.all_to_all(sums, ('z', 'y'), 0, 0, tiled=True)  21.9 us
    pallas_call x1, Pallas kernels, react(): pl.pallas_call(react_kernel, out_shape=jax.ShapeDtypeStruct((FLOW, NQ * S...  13.8 us
    all_to_all x1, waiting for transfers between devices, body(): recv = lax.all_to_all(send, ('z', 'y'), 0, 0, tiled=True)  11.5 us
    all_to_all x1, starting transfers between devices, body(): recv = lax.all_to_all(send, ('z', 'y'), 0, 0, tiled=True)  8.28 us
    ppermute x1, starting transfers between devices, body(): message = lax.ppermute(message, everywhere, route)  3.5 us
    ppermute x1, waiting for transfers between devices, body(): lanes = lax.ppermute(locate(recv, slots), everywhere, route)  3.16 us
    pallas_call x1, Pallas kernels, cells_to_send(): pl.pallas_call(cells_kernel, out_shape=jax.ShapeDtypeStruct((FLOW, (NC +...  1.99 us
    ppermute x1, starting transfers between devices, body(): lanes = lax.ppermute(locate(recv, slots), everywhere, route)  1.55 us
  transfers between devices with their start and end apart: 3, of which 2 were waited for; matrix products, arithmetic and copies ran while one was open for 0% of the time, Pallas kernels for 2%

profile of v6, /device:TPU:0, one launch (start us, length us, event | category | flops | bytes accessed | tf_op | source)
XLA Modules:
  0.0 68.2 jit_solution(11882837332591664413)
XLA Ops:
  0.0 2.0 %cells.1 = f32[16,104,128]{2,1,0:T(8,128)} custom-call(s32[1]{0:T(128)} %bitcast.column_ref, f32[12,32768]{1,0:T(8,128)} %cell_ref.1, s32[1,1,16,1024]{3,2,1,0:T(8,128)} %pick_ref.1), custom_call_target="tpu_custom_call" | custom-call | tf_op jit(solution)/shard_map/cells/pallas_call | solution.py:113
  2.0 0.0 copy-start
  2.0 0.0 copy-start.1
  2.0 0.0 copy-start.3
  2.0 0.0 copy-start.2
  2.0 0.0 copy-start.4
  2.0 8.3 %all-to-all-start = ((f32[16,104,128]{2,1,0:T(8,128)}), f32[16,104,128]{2,1,0:T(8,128)S(1)}, u32[]{:S(2)}, u32[]{:S(2)}) async-start(f32[16,104,128]{2,1,0:T(8,128)} %cells.1), calls=%async_computation | async-start | bytes 1703936 | tf_op jit(solution)/shard_map/all_to_all | solution.py:408
  10.3 0.0 copy-done
  10.3 0.0 copy-done.1
  10.3 0.0 copy-done.3
  10.3 0.2 pack.1
  10.6 3.5 %collective-permute-start.1 = (f32[144,128]{1,0:T(8,128)S(1)}, f32[144,128]{1,0:T(8,128)S(1)}, u32[]{:S(2)}, u32[]{:S(2)}) collective-permute-start(f32[144,128]{1,0:T(8,128)S(1)} %get-tuple-element.11), channel_id=1, source_target_pairs={{0,64},{1,4},{2,32},{3,100},{4,0},{5,68},{6,96},{7,36},{8,72},{9,1... | collective-permute-start | bytes 221192 | tf_op jit(solution)/shard_map/ppermute | solution.py:410
  14.1 11.5 %all-to-all-done.recv_ref = f32[16,104,128]{2,1,0:T(8,128)S(1)} async-done(((f32[16,104,128]{2,1,0:T(8,128)}), f32[16,104,128]{2,1,0:T(8,128)S(1)}, u32[]{:S(2)}, u32[]{:S(2)}) %all-to-all-start) | async-done | bytes 852000 | tf_op jit(solution)/shard_map/all_to_all | solution.py:408
  25.6 0.1 locate.1
  25.7 1.6 %collective-permute-start = (f32[128,128]{1,0:T(8,128)S(1)}, f32[128,128]{1,0:T(8,128)S(1)}, u32[]{:S(2)}, u32[]{:S(2)}) collective-permute-start(f32[128,128]{1,0:T(8,128)S(1)} %locate.1), channel_id=1, source_target_pairs={{0,64},{1,4},{2,32},{3,100},{4,0},{5,68},{6,96},{7,36},{8,72},{9,1... | collective-permute-start | bytes 196616 | tf_op jit(solution)/shard_map/ppermute | solution.py:411
  27.2 0.0 copy-done.2
  27.2 1.2 %tables.1 = (bf16[176,576]{1,0:T(8,128)(2,1)S(1)}, bf16[624,240]{1,0:T(8,128)(2,1)S(1)}, bf16[96,288]{1,0:T(8,128)(2,1)S(1)}) custom-call(f32[6,12]{1,0:T(8,128)S(1)} %copy-done.2), custom_call_target="tpu_custom_call" | custom-call | tf_op jit(solution)/shard_map/tables/pallas_call | solution.py:81
  28.4 0.0 collective-permute-done.1.message_ref
  28.4 3.2 %collective-permute-done.lanes_ref = f32[128,128]{1,0:T(8,128)S(1)} collective-permute-done((f32[128,128]{1,0:T(8,128)S(1)}, f32[128,128]{1,0:T(8,128)S(1)}, u32[]{:S(2)}, u32[]{:S(2)}) %collective-permute-start) | collective-permute-done | bytes 65568 | tf_op jit(solution)/shard_map/ppermute | solution.py:411
  31.6 0.0 copy-done.4
  31.6 13.8 %react.1 = f32[16,152,128]{2,1,0:T(8,128)S(1)} custom-call(f32[16,104,128]{2,1,0:T(8,128)S(1)} %all-to-all-done.recv_ref, f32[128,128]{1,0:T(8,128)S(1)} %collective-permute-done.lanes_ref, f32[144,128]{1,0:T(8,128)S(1)} %collective-permute-done.1.message_ref, bf16[176,576]{1,0:T(8,128)(2,1)S(1)} %get-tuple-element.12.gram_ref, ...), custom_call_target="tpu_custom_call" | custom-call | tf_op jit(solution)/shard_map/react/pallas_call | solution.py:379
  45.4 21.9 %all_to_all.10.sums_ref = f32[16,152,128]{2,1,0:T(8,128)S(1)} all-to-all(f32[16,152,128]{2,1,0:T(8,128)S(1)} %react.1), channel_id=1, replica_groups=mesh['z'=4,'y'=4,'h'=2,'q'=4] {'z','y'}, dimensions={0} | all-to-all | bytes 2490368 | tf_op jit(solution)/shard_map/all_to_all | solution.py:413
  67.3 0.9 %mean.1 = f32[18,4096]{1,0:T(8,128)} custom-call(f32[16,152,128]{2,1,0:T(8,128)S(1)} %all_to_all.10.sums_ref), custom_call_target="tpu_custom_call" | custom-call | tf_op jit(solution)/shard_map/mean/pallas_call | solution.py:199
Async XLA Ops:
  2.0 8.3 %copy-start = (s32[256,64]{0,1:T(8,128)S(1)}, s32[256,64]{0,1:T(8,128)}, u32[]{:S(2)}) copy-start(s32[256,64]{0,1:T(8,128)} %param.11) | copy-start | bytes 196612
  2.0 8.3 %copy-start.1 = (f32[256,64]{0,1:T(8,128)S(1)}, f32[256,64]{0,1:T(8,128)}, u32[]{:S(2)}) copy-start(f32[256,64]{0,1:T(8,128)} %param.9) | copy-start | bytes 196612
  2.0 8.3 %copy-start.3 = (f32[12,64]{1,0:T(8,128)S(1)}, f32[12,64]{1,0:T(8,128)}, u32[]{:S(2)}) copy-start(f32[12,64]{1,0:T(8,128)} %inflow_ref.1) | copy-start | bytes 9220
  2.0 25.2 %copy-start.2 = (f32[6,12]{1,0:T(8,128)S(1)}, f32[6,12]{1,0:T(8,128)}, u32[]{:S(2)}) copy-start(f32[6,12]{1,0:T(8,128)} %stoich_ref.3) | copy-start | bytes 868
  2.0 29.6 %copy-start.4 = (f32[6]{0:T(128)S(1)}, f32[6]{0:T(128)}, u32[]{:S(2)}) copy-start(f32[6]{0:T(128)} %logk_ref.1) | copy-start | bytes 76
  2.0 23.6 %all-to-all-start = ((f32[16,104,128]{2,1,0:T(8,128)}), f32[16,104,128]{2,1,0:T(8,128)S(1)}, u32[]{:S(2)}, u32[]{:S(2)}) async-start(f32[16,104,128]{2,1,0:T(8,128)} %cells.1), calls=%async_computation | async-start | bytes 1703936 | tf_op jit(solution)/shard_map/all_to_all | solution.py:408
  10.6 17.9 %collective-permute-start.1 = (f32[144,128]{1,0:T(8,128)S(1)}, f32[144,128]{1,0:T(8,128)S(1)}, u32[]{:S(2)}, u32[]{:S(2)}) collective-permute-start(f32[144,128]{1,0:T(8,128)S(1)} %get-tuple-element.11), channel_id=1, source_target_pairs={{0,64},{1,4},{2,32},{3,100},{4,0},{5,68},{6,96},{7,36},{8,72},{9,1... | collective-permute-start | bytes 221192 | tf_op jit(solution)/shard_map/ppermute | solution.py:410
  25.7 5.9 %collective-permute-start = (f32[128,128]{1,0:T(8,128)S(1)}, f32[128,128]{1,0:T(8,128)S(1)}, u32[]{:S(2)}, u32[]{:S(2)}) collective-permute-start(f32[128,128]{1,0:T(8,128)S(1)} %locate.1), channel_id=1, source_target_pairs={{0,64},{1,4},{2,32},{3,100},{4,0},{5,68},{6,96},{7,36},{8,72},{9,1... | collective-permute-start | bytes 196616 | tf_op jit(solution)/shard_map/ppermute | solution.py:411

commit v7 on v6

--- a/solution.py
+++ b/solution.py
@@ -120,12 +120,13 @@
                 pl.BlockSpec((NC, block), lambda step, column: (0, column[0])),
                 pl.BlockSpec((1, 1, FLOW, SUB * WIN), lambda step, column: (0, 0, 0, 0)),
             ],
-            out_specs=pl.BlockSpec((FLOW, (NC + 1) * SUB, WIN), lambda step, column: (0, 0, 0)),
+            out_specs=pl.BlockSpec(memory_space=pltpu.VMEM),
             scratch_shapes=[
                 pltpu.VMEM((FLOW * SUB, WIN), F32),
                 pltpu.VMEM((SIDE, FLOW * SUB, WIN), F32),
             ],
         ),
+        compiler_params=pltpu.CompilerParams(vmem_limit_bytes=125 * 512 * 1024),
         name="cells",
     )(column, cell_state, pick)
 

time: 69.2 us -> 69.2 us (level)
  no operation moved by 1% of the time
where the time goes in v7:
time: 69.2 us; the launch traced here: 68.2 us
  blocking collectives  21.9 us (32%)
  Pallas kernels  18.1 us (26%)
  waiting for transfers between devices  14.7 us (21%)
  starting transfers between devices  13.3 us (19%)
    all_to_all x1, blocking collectives, body(): back = lax.all_to_all(sums, ('z', 'y'), 0, 0, tiled=True)  21.9 us
    pallas_call x1, Pallas kernels, react(): pl.pallas_call(react_kernel, out_shape=jax.ShapeDtypeStruct((FLOW, NQ * S...  13.8 us
    all_to_all x1, waiting for transfers between devices, body(): recv = lax.all_to_all(send, ('z', 'y'), 0, 0, tiled=True)  11.5 us
    all_to_all x1, starting transfers between devices, body(): recv = lax.all_to_all(send, ('z', 'y'), 0, 0, tiled=True)  8.28 us
    ppermute x1, starting transfers between devices, body(): message = lax.ppermute(message, everywhere, route)  3.5 us
    ppermute x1, waiting for transfers between devices, body(): lanes = lax.ppermute(locate(recv, slots), everywhere, route)  3.16 us
    pallas_call x1, Pallas kernels, cells_to_send(): pl.pallas_call(cells_kernel, out_shape=jax.ShapeDtypeStruct((FLOW, (NC +...  1.99 us
    ppermute x1, starting transfers between devices, body(): lanes = lax.ppermute(locate(recv, slots), everywhere, route)  1.55 us
  transfers between devices with their start and end apart: 3, of which 2 were waited for; matrix products, arithmetic and copies ran while one was open for 0% of the time, Pallas kernels for 2%

profile of v7, /device:TPU:0, one launch (start us, length us, event | category | flops | bytes accessed | tf_op | source)
XLA Modules:
  0.0 68.2 jit_solution(11882837332591664413)
XLA Ops:
  0.0 2.0 %cells.1 = f32[16,104,128]{2,1,0:T(8,128)} custom-call(s32[1]{0:T(128)} %bitcast.column_ref, f32[12,32768]{1,0:T(8,128)} %cell_ref.1, s32[1,1,16,1024]{3,2,1,0:T(8,128)} %pick_ref.1), custom_call_target="tpu_custom_call" | custom-call | tf_op jit(solution)/shard_map/cells/pallas_call | solution.py:113
  2.0 0.0 copy-start
  2.0 0.0 copy-start.1
  2.0 0.0 copy-start.3
  2.0 0.0 copy-start.2
  2.0 0.0 copy-start.4
  2.0 8.3 %all-to-all-start = ((f32[16,104,128]{2,1,0:T(8,128)}), f32[16,104,128]{2,1,0:T(8,128)S(1)}, u32[]{:S(2)}, u32[]{:S(2)}) async-start(f32[16,104,128]{2,1,0:T(8,128)} %cells.1), calls=%async_computation | async-start | bytes 1703936 | tf_op jit(solution)/shard_map/all_to_all | solution.py:409
  10.3 0.0 copy-done
  10.3 0.0 copy-done.1
  10.3 0.0 copy-done.3
  10.3 0.2 pack.1
  10.6 3.5 %collective-permute-start.1 = (f32[144,128]{1,0:T(8,128)S(1)}, f32[144,128]{1,0:T(8,128)S(1)}, u32[]{:S(2)}, u32[]{:S(2)}) collective-permute-start(f32[144,128]{1,0:T(8,128)S(1)} %get-tuple-element.11), channel_id=1, source_target_pairs={{0,64},{1,4},{2,32},{3,100},{4,0},{5,68},{6,96},{7,36},{8,72},{9,1... | collective-permute-start | bytes 221192 | tf_op jit(solution)/shard_map/ppermute | solution.py:411
  14.1 11.5 %all-to-all-done.recv_ref = f32[16,104,128]{2,1,0:T(8,128)S(1)} async-done(((f32[16,104,128]{2,1,0:T(8,128)}), f32[16,104,128]{2,1,0:T(8,128)S(1)}, u32[]{:S(2)}, u32[]{:S(2)}) %all-to-all-start) | async-done | bytes 852000 | tf_op jit(solution)/shard_map/all_to_all | solution.py:409
  25.6 0.1 locate.1
  25.7 1.6 %collective-permute-start = (f32[128,128]{1,0:T(8,128)S(1)}, f32[128,128]{1,0:T(8,128)S(1)}, u32[]{:S(2)}, u32[]{:S(2)}) collective-permute-start(f32[128,128]{1,0:T(8,128)S(1)} %locate.1), channel_id=1, source_target_pairs={{0,64},{1,4},{2,32},{3,100},{4,0},{5,68},{6,96},{7,36},{8,72},{9,1... | collective-permute-start | bytes 196616 | tf_op jit(solution)/shard_map/ppermute | solution.py:412
  27.2 0.0 copy-done.2
  27.2 1.2 %tables.1 = (bf16[176,576]{1,0:T(8,128)(2,1)S(1)}, bf16[624,240]{1,0:T(8,128)(2,1)S(1)}, bf16[96,288]{1,0:T(8,128)(2,1)S(1)}) custom-call(f32[6,12]{1,0:T(8,128)S(1)} %copy-done.2), custom_call_target="tpu_custom_call" | custom-call | tf_op jit(solution)/shard_map/tables/pallas_call | solution.py:81
  28.4 0.0 collective-permute-done.1.message_ref
  28.4 3.2 %collective-permute-done.lanes_ref = f32[128,128]{1,0:T(8,128)S(1)} collective-permute-done((f32[128,128]{1,0:T(8,128)S(1)}, f32[128,128]{1,0:T(8,128)S(1)}, u32[]{:S(2)}, u32[]{:S(2)}) %collective-permute-start) | collective-permute-done | bytes 65568 | tf_op jit(solution)/shard_map/ppermute | solution.py:412
  31.6 0.0 copy-done.4
  31.6 13.8 %react.1 = f32[16,152,128]{2,1,0:T(8,128)S(1)} custom-call(f32[16,104,128]{2,1,0:T(8,128)S(1)} %all-to-all-done.recv_ref, f32[128,128]{1,0:T(8,128)S(1)} %collective-permute-done.lanes_ref, f32[144,128]{1,0:T(8,128)S(1)} %collective-permute-done.1.message_ref, bf16[176,576]{1,0:T(8,128)(2,1)S(1)} %get-tuple-element.12.gram_ref, ...), custom_call_target="tpu_custom_call" | custom-call | tf_op jit(solution)/shard_map/react/pallas_call | solution.py:380
  45.4 21.9 %all_to_all.10.sums_ref = f32[16,152,128]{2,1,0:T(8,128)S(1)} all-to-all(f32[16,152,128]{2,1,0:T(8,128)S(1)} %react.1), channel_id=1, replica_groups=mesh['z'=4,'y'=4,'h'=2,'q'=4] {'z','y'}, dimensions={0} | all-to-all | bytes 2490368 | tf_op jit(solution)/shard_map/all_to_all | solution.py:414
  67.3 0.9 %mean.1 = f32[18,4096]{1,0:T(8,128)} custom-call(f32[16,152,128]{2,1,0:T(8,128)S(1)} %all_to_all.10.sums_ref), custom_call_target="tpu_custom_call" | custom-call | tf_op jit(solution)/shard_map/mean/pallas_call | solution.py:200
Async XLA Ops:
  2.0 8.3 %copy-start = (s32[256,64]{0,1:T(8,128)S(1)}, s32[256,64]{0,1:T(8,128)}, u32[]{:S(2)}) copy-start(s32[256,64]{0,1:T(8,128)} %param.11) | copy-start | bytes 196612
  2.0 8.3 %copy-start.1 = (f32[256,64]{0,1:T(8,128)S(1)}, f32[256,64]{0,1:T(8,128)}, u32[]{:S(2)}) copy-start(f32[256,64]{0,1:T(8,128)} %param.9) | copy-start | bytes 196612
  2.0 8.3 %copy-start.3 = (f32[12,64]{1,0:T(8,128)S(1)}, f32[12,64]{1,0:T(8,128)}, u32[]{:S(2)}) copy-start(f32[12,64]{1,0:T(8,128)} %inflow_ref.1) | copy-start | bytes 9220
  2.0 25.2 %copy-start.2 = (f32[6,12]{1,0:T(8,128)S(1)}, f32[6,12]{1,0:T(8,128)}, u32[]{:S(2)}) copy-start(f32[6,12]{1,0:T(8,128)} %stoich_ref.3) | copy-start | bytes 868
  2.0 29.6 %copy-start.4 = (f32[6]{0:T(128)S(1)}, f32[6]{0:T(128)}, u32[]{:S(2)}) copy-start(f32[6]{0:T(128)} %logk_ref.1) | copy-start | bytes 76
  2.0 23.6 %all-to-all-start = ((f32[16,104,128]{2,1,0:T(8,128)}), f32[16,104,128]{2,1,0:T(8,128)S(1)}, u32[]{:S(2)}, u32[]{:S(2)}) async-start(f32[16,104,128]{2,1,0:T(8,128)} %cells.1), calls=%async_computation | async-start | bytes 1703936 | tf_op jit(solution)/shard_map/all_to_all | solution.py:409
  10.6 17.9 %collective-permute-start.1 = (f32[144,128]{1,0:T(8,128)S(1)}, f32[144,128]{1,0:T(8,128)S(1)}, u32[]{:S(2)}, u32[]{:S(2)}) collective-permute-start(f32[144,128]{1,0:T(8,128)S(1)} %get-tuple-element.11), channel_id=1, source_target_pairs={{0,64},{1,4},{2,32},{3,100},{4,0},{5,68},{6,96},{7,36},{8,72},{9,1... | collective-permute-start | bytes 221192 | tf_op jit(solution)/shard_map/ppermute | solution.py:411
  25.7 5.9 %collective-permute-start = (f32[128,128]{1,0:T(8,128)S(1)}, f32[128,128]{1,0:T(8,128)S(1)}, u32[]{:S(2)}, u32[]{:S(2)}) collective-permute-start(f32[128,128]{1,0:T(8,128)S(1)} %locate.1), channel_id=1, source_target_pairs={{0,64},{1,4},{2,32},{3,100},{4,0},{5,68},{6,96},{7,36},{8,72},{9,1... | collective-permute-start | bytes 196616 | tf_op jit(solution)/shard_map/ppermute | solution.py:412
